TPU v7x, 512 devices: a whole 4x4x16 slice. The times are simulated.
512 devices in a mesh: node: 16 (over x, z_hi), local: 32 (over z_lo, y, core).
Axes of the slice: x: 4, y: 4, z: 16 (z_hi: 4, z_lo: 4; z = z_hi * 4 + z_lo), core: 2. Of those that a mesh axis runs over, the one named last changes fastest.
Arguments:
- activations: bfloat16 [98304, 2560], P(('node', 'local')), may hold values from -0.078125 to 0.078125
- out_grad: bfloat16 [98304, 512], P(('node', 'local')), may hold values from -6 to 6
- key_weight: bfloat16 [2560, 512], P('local'), may hold values from -0.125 to 0.125
Outputs:
- input_grad: bfloat16 [98304, 2560], P(('node', 'local'))
- weight_grad: float32 [2560, 512], P(('node', 'local'))
All inputs are finite; a program needn't handle non-finite values.
Results may differ from a plain program's by a relative error of at most 0.0049.
Values may be sent and summed in bfloat16 or wider, within the bound.
No kernel may reach another device: no remote copies, remote signals or barrier semaphores. Data moves between devices by JAX's collectives and lax.ppermute only.
A program may use at most 128 MiB of HBM per device.

v0:
```python
import jax
import jax.numpy as jnp
from jax import lax
from jax.sharding import PartitionSpec as P

BLOCK = 256


def encode_blocks(grad):
    blocks = grad.reshape(grad.shape[:-1] + (grad.shape[-1] // BLOCK, BLOCK))
    scales = (jnp.max(jnp.abs(blocks), axis=-1) / 7.0 + 1e-06).astype(jnp.bfloat16)
    coded = (blocks / scales.astype(jnp.float32)[..., None]).astype(jnp.bfloat16)
    return (coded.reshape(grad.shape), scales)


def decode_blocks(coded, scales):
    blocks = coded.astype(jnp.float32).reshape(coded.shape[:-1] + (coded.shape[-1] // BLOCK, BLOCK))
    return (blocks * scales.astype(jnp.float32)[..., None]).reshape(coded.shape)


def body(activations, out_grad, key_weight):
    n_local = lax.axis_size("local")
    n_node = lax.axis_size("node")
    product = lax.dot_general(
        out_grad,
        lax.all_gather(key_weight, "local", axis=0, tiled=True),
        (((1,), (1,)), ((), ())),
        preferred_element_type=jnp.float32,
    )
    input_grad = product.astype(jnp.bfloat16)
    partial_value = lax.dot_general(
        activations, out_grad, (((0,), (0,)), ((), ())), preferred_element_type=jnp.float32
    )
    row_count = partial_value.shape[0] // (n_node * n_local)
    shaped = partial_value.reshape(n_node, n_local, row_count, partial_value.shape[1])
    coded, scales = encode_blocks(shaped)
    coded, scales = (
        lax.all_to_all(coded, "local", split_axis=1, concat_axis=1, tiled=True),
        lax.all_to_all(scales, "local", split_axis=1, concat_axis=1, tiled=True),
    )
    group_sum = jnp.sum(decode_blocks(coded, scales), axis=1)
    coded, scales = encode_blocks(group_sum)
    coded, scales = (
        lax.all_to_all(coded, "node", split_axis=0, concat_axis=0, tiled=True),
        lax.all_to_all(scales, "node", split_axis=0, concat_axis=0, tiled=True),
    )
    weight_grad = jnp.sum(decode_blocks(coded, scales), axis=0)
    return (input_grad, weight_grad)


def solution(mesh):
    placed = (P(("node", "local"), None), P(("node", "local"), None), P("local", None))
    return jax.shard_map(
        body,
        mesh=mesh,
        in_specs=placed,
        out_specs=(P(("node", "local"), None), P(("node", "local"), None)),
        check_vma=False,
    )
```

profile of v0, /device:TPU:1, one launch (start us, length us, event | category | flops | bytes accessed | tf_op | source)
XLA Modules:
  0.0 211.4 jit_solution(5506031310775103665)
XLA Ops:
  7.2 1.2 copy-done
  8.4 5.7 %fusion.2 = (f32[2560,512]{1,0:T(8,128)}, f32[2560,512]{1,0:T(8,128)}) fusion(bf16[192,2560]{1,0:T(8,128)(2,1)S(1)} %copy-done, bf16[192,512]{1,0:T(8,128)(2,1)} %param.4), kind=kOutput, calls=%fused_computation.10 | convolution fusion | flops 504627200 | bytes 11665408 | tf_op jit(solution)/shard_map/dot_general | solution.py:31
  14.0 7.5 %abs.13 = f32[16,32,5,2,256]{4,3,2,1,0:T(2,128)} reshape(f32[2560,512]{1,0:T(8,128)} %get-tuple-element.2) | data formatting | bytes 10485760 | tf_op jit(solution)/shard_map/abs | solution.py:11
  21.5 5.4 %reduce_max.18 = f32[16,32,5,2]{3,2,1,0:T(8,128)S(1)} reduce(f32[16,32,5,2,256]{4,3,2,1,0:T(2,128)} %abs.13, f32[]{:T(128)} %constant.4.clone.1), dimensions={4}, to_apply=%region_0.0 | reduce | flops 1305600 | bytes 5263364 | tf_op jit(solution)/shard_map/reduce_max | solution.py:11
  26.9 0.7 copy.31
  27.6 0.8 copy.36
  28.3 10.4 %all-to-all-start.1 = ((bf16[16,32,5,2]{0,3,2,1:T(2,128)(2,1)}), bf16[16,32,5,2]{0,3,2,1:T(2,128)(2,1)S(1)}, u32[]{:S(2)}, u32[]{:S(2)}) async-start(bf16[16,32,5,2]{0,3,2,1:T(2,128)(2,1)} %copy.36), calls=%async_computation.1 | async-start | bytes 163840 | tf_op jit(solution)/shard_map/all_to_all | solution.py:39
  38.8 0.6 copy.32
  39.3 4.8 %div.36 = f32[16,32,5,2,256]{4,3,1,2,0:T(2,128)} broadcast(f32[16,32,5,2]{3,1,2,0:T(8,128)S(1)} %copy.32), dimensions={0,1,2,3} | broadcast | bytes 5263360 | tf_op jit(solution)/shard_map/div | solution.py:12
  44.1 8.0 %div.37 = f32[16,32,5,512]{3,1,2,0:T(8,128)} reshape(f32[16,32,5,2,256]{4,3,1,2,0:T(2,128)} %div.36) | data formatting | bytes 10485760 | tf_op jit(solution)/shard_map/div | solution.py:12
  52.1 7.4 %reshape_reshape.3 = f32[16,32,5,512]{3,2,1,0:T(8,128)} reshape(f32[2560,512]{1,0:T(8,128)} %get-tuple-element.3) | data formatting | bytes 10485760 | tf_op jit(solution)/shard_map/reshape;reshape | solution.py:10
  59.5 8.4 %fusion = bf16[16,32,5,512]{3,1,2,0:T(8,128)(2,1)S(1)} fusion(f32[16,32,5,512]{3,1,2,0:T(8,128)} %div.37, f32[16,32,5,512]{3,2,1,0:T(8,128)} %reshape_reshape.3), kind=kLoop, calls=%fused_computation.1 | loop fusion | flops 2621440 | bytes 13107200 | tf_op jit(solution)/shard_map/convert_element_type | solution.py:12
  67.9 3.0 %copy.34 = bf16[16,32,5,512]{3,0,2,1:T(8,128)(2,1)} copy(bf16[16,32,5,512]{3,1,2,0:T(8,128)(2,1)S(1)} %fusion) | data formatting | bytes 5242880 | tf_op jit(solution)/shard_map/convert_element_type | solution.py:12
  70.8 7.9 %all-to-all-start = ((bf16[16,32,5,512]{3,0,2,1:T(8,128)(2,1)}), bf16[16,32,5,512]{3,0,2,1:T(8,128)(2,1)}, u32[]{:S(2)}, u32[]{:S(2)}) async-start(bf16[16,32,5,512]{3,0,2,1:T(8,128)(2,1)} %copy.34), calls=%async_computation | async-start | bytes 5242880 | tf_op jit(solution)/shard_map/all_to_all | solution.py:38
  78.7 0.3 all-gather.2.cloned.1.call-start
  79.0 0.5 all-gather.2.cloned.1.call-update
  79.6 0.6 copy.38
  80.2 4.9 %mul.22 = f32[16,32,5,2,256]{4,3,1,2,0:T(2,128)} broadcast(f32[16,32,5,2]{3,1,2,0:T(8,128)S(1)} %copy.38), dimensions={0,1,2,3} | broadcast | bytes 5263360 | tf_op jit(solution)/shard_map/mul | solution.py:18
  85.0 8.0 %mul.23 = f32[16,32,5,512]{3,1,2,0:T(8,128)} reshape(f32[16,32,5,2,256]{4,3,1,2,0:T(2,128)} %mul.22) | data formatting | bytes 10485760 | tf_op jit(solution)/shard_map/mul | solution.py:18
  93.0 55.7 %all-to-all-done = bf16[16,32,5,512]{3,0,2,1:T(8,128)(2,1)} async-done(((bf16[16,32,5,512]{3,0,2,1:T(8,128)(2,1)}), bf16[16,32,5,512]{3,0,2,1:T(8,128)(2,1)}, u32[]{:S(2)}, u32[]{:S(2)}) %all-to-all-start) | async-done | bytes 2621472 | tf_op jit(solution)/shard_map/all_to_all | solution.py:38
  148.7 5.5 %multiply_reduce_fusion = f32[16,5,512]{2,1,0:T(8,128)S(1)} fusion(f32[16,32,5,512]{3,1,2,0:T(8,128)} %mul.23, bf16[16,32,5,512]{3,0,2,1:T(8,128)(2,1)} %all-to-all-done), kind=kLoop, calls=%fused_computation.2 | loop fusion | flops 3891200 | bytes 8028160 | tf_op jit(solution)/shard_map/reduce_sum | solution.py:41
  154.4 0.2 reduce_max.19
  154.8 0.7 copy.45
  155.5 0.1 div.41
  155.8 14.6 %all-to-all-start.3 = ((bf16[16,5,2]{1,2,0:T(2,128)(2,1)}), bf16[16,5,2]{1,2,0:T(2,128)(2,1)S(1)}, u32[]{:S(2)}, u32[]{:S(2)}) async-start(bf16[16,5,2]{1,2,0:T(2,128)(2,1)} %copy.45), calls=%async_computation.3 | async-start | bytes 16384 | tf_op jit(solution)/shard_map/all_to_all | solution.py:45
  170.4 0.8 fusion.1
  171.2 12.8 %all-to-all-done.3 = bf16[16,5,2]{1,2,0:T(2,128)(2,1)S(1)} async-done(((bf16[16,5,2]{1,2,0:T(2,128)(2,1)}), bf16[16,5,2]{1,2,0:T(2,128)(2,1)S(1)}, u32[]{:S(2)}, u32[]{:S(2)}) %all-to-all-start.3) | async-done | bytes 352 | tf_op jit(solution)/shard_map/all_to_all | solution.py:45
  184.0 3.5 %all-to-all-start.2 = ((bf16[16,5,512]{2,1,0:T(8,128)(2,1)}), bf16[16,5,512]{2,1,0:T(8,128)(2,1)S(1)}, u32[]{:S(2)}, u32[]{:S(2)}) async-start(bf16[16,5,512]{2,1,0:T(8,128)(2,1)} %fusion.1), calls=%async_computation.2 | async-start | bytes 262144 | tf_op jit(solution)/shard_map/all_to_all | solution.py:44
  187.5 3.7 %convolution_convert_fusion = bf16[192,2560]{1,0:T(8,128)(2,1)} fusion(bf16[192,512]{1,0:T(8,128)(2,1)S(1)} %copy-done.1, bf16[2560,512]{1,0:T(8,128)(2,1)} %all-gather.2.cloned.1.call-done), kind=kOutput, calls=%fused_computation.3 | convolution fusion | flops 503808000 | bytes 3801088 | tf_op jit(solution)/shard_map/dot_general | solution.py:24
  191.5 0.1 mul.25
  191.7 12.2 %all-to-all-done.2 = bf16[16,5,512]{2,1,0:T(8,128)(2,1)S(1)} async-done(((bf16[16,5,512]{2,1,0:T(8,128)(2,1)}), bf16[16,5,512]{2,1,0:T(8,128)(2,1)S(1)}, u32[]{:S(2)}, u32[]{:S(2)}) %all-to-all-start.2) | async-done | bytes 81952 | tf_op jit(solution)/shard_map/all_to_all | solution.py:44
  203.9 0.7 multiply_reduce_fusion.1
  (16 shorter events, 1.1 us)
Async XLA Ops:
  7.2 1.2 copy-start
  28.3 42.5 %all-to-all-start.1 = ((bf16[16,32,5,2]{0,3,2,1:T(2,128)(2,1)}), bf16[16,32,5,2]{0,3,2,1:T(2,128)(2,1)S(1)}, u32[]{:S(2)}, u32[]{:S(2)}) async-start(bf16[16,32,5,2]{0,3,2,1:T(2,128)(2,1)} %copy.36), calls=%async_computation.1 | async-start | bytes 163840 | tf_op jit(solution)/shard_map/all_to_all | solution.py:39
  70.8 77.9 %all-to-all-start = ((bf16[16,32,5,512]{3,0,2,1:T(8,128)(2,1)}), bf16[16,32,5,512]{3,0,2,1:T(8,128)(2,1)}, u32[]{:S(2)}, u32[]{:S(2)}) async-start(bf16[16,32,5,512]{3,0,2,1:T(8,128)(2,1)} %copy.34), calls=%async_computation | async-start | bytes 5242880 | tf_op jit(solution)/shard_map/all_to_all | solution.py:38
  78.7 108.8 %all-gather.2.cloned.1.call-start = ((), (), s32[]{:S(2)}) async-start(), calls=%async_computation.4 | async-start | bytes 2703360 | tf_op jit(solution)/shard_map/all_gather | solution.py:26
  93.0 94.6 %copy-start.1 = (bf16[192,512]{1,0:T(8,128)(2,1)S(1)}, bf16[192,512]{1,0:T(8,128)(2,1)}, u32[]{:S(2)}) copy-start(bf16[192,512]{1,0:T(8,128)(2,1)} %param.4) | copy-start | bytes 589828
  155.8 28.2 %all-to-all-start.3 = ((bf16[16,5,2]{1,2,0:T(2,128)(2,1)}), bf16[16,5,2]{1,2,0:T(2,128)(2,1)S(1)}, u32[]{:S(2)}, u32[]{:S(2)}) async-start(bf16[16,5,2]{1,2,0:T(2,128)(2,1)} %copy.45), calls=%async_computation.3 | async-start | bytes 16384 | tf_op jit(solution)/shard_map/all_to_all | solution.py:45
  184.0 19.9 %all-to-all-start.2 = ((bf16[16,5,512]{2,1,0:T(8,128)(2,1)}), bf16[16,5,512]{2,1,0:T(8,128)(2,1)S(1)}, u32[]{:S(2)}, u32[]{:S(2)}) async-start(bf16[16,5,512]{2,1,0:T(8,128)(2,1)} %fusion.1), calls=%async_computation.2 | async-start | bytes 262144 | tf_op jit(solution)/shard_map/all_to_all | solution.py:44
Sparse Core Ops, SparseCore 0:
  81.7 79.8 all-gather.1
where the time goes:
time: 212 us; the launch traced here: 211 us
  waiting for transfers between devices  81.2 us (38%)
  local copies, waits for them, and re-layouts  49 us (23%)
  starting transfers between devices  36.7 us (17%)
  other arithmetic  20.9 us (10%)
  between operations  14.2 us (7%)
  matrix products  9.37 us (4%)
    all_to_all x1, waiting for transfers between devices, body(): lax.all_to_all(coded, 'local', split_axis=1, concat_axis=1, tiled=True)  55.7 us
    all_to_all x1, starting transfers between devices, body(): lax.all_to_all(scales, 'node', split_axis=0, concat_axis=0, tiled=True)  14.6 us
    div x4, local copies, waits for them, and re-layouts, encode_blocks(): blocks / scales.astype(jnp.float32)[..., None]  13.1 us
    mul x4, local copies, waits for them, and re-layouts, decode_blocks(): return (blocks * scales.astype(jnp.float32)[..., None]).reshape(coded.shape)  13.1 us
    all_to_all x1, waiting for transfers between devices, body(): lax.all_to_all(scales, 'node', split_axis=0, concat_axis=0, tiled=True)  12.8 us
    all_to_all x1, waiting for transfers between devices, body(): lax.all_to_all(coded, 'node', split_axis=0, concat_axis=0, tiled=True)  12.2 us
    all_to_all x1, starting transfers between devices, body(): lax.all_to_all(scales, 'local', split_axis=1, concat_axis=1, tiled=True)  10.4 us
    convert_element_type x2, other arithmetic, encode_blocks(): (blocks / scales.astype(jnp.float32)[..., None]).astype(jnp.bfloat16)  9.14 us
  transfers between devices with their start and end apart: 5, of which 3 were waited for; matrix products, arithmetic and copies ran while one was open for 27% of the time, Pallas kernels for 0%

commit v1 on v0

v1 whole, which is shorter than its diff:
```python
import jax
import jax.numpy as jnp
from jax import lax
from jax.experimental import pallas as pl
from jax.experimental.pallas import tpu as pltpu
from jax.sharding import Mesh, PartitionSpec as P

X, ZH, ZL, Y, C = 4, 4, 4, 4, 2
Z = ZH * ZL
VMEM_LIMIT = 48 * 1024 * 1024

NT = (((1,), (1,)), ((), ()))
TN = (((0,), (0,)), ((), ()))


def dot(a, b, dims):
    return lax.dot_general(a, b, dims, preferred_element_type=jnp.float32)


def all_to_all(a, axes):
    return lax.all_to_all(a, axes, split_axis=0, concat_axis=0, tiled=True)


def shift(a, axes, step, size):
    return lax.ppermute(a, axes, [(i, (i + step) % size) for i in range(size)])


def pair_product(act, act_other, grad, grad_other, out):
    half = pl.ds(pl.multiple_of(lax.axis_index("c") * 256, 256), 256)
    total = dot(grad[:, half], act[...], TN) + dot(grad_other[:, half], act_other[...], TN)
    rows = out.shape[0]
    source = lax.broadcasted_iota(jnp.int32, (1, rows), 1)
    tens = (source * 6554) >> 16
    place = (tens & 3) * (10 * Z) + (tens >> 2) * 10 + (source - tens * 10)
    target = lax.broadcasted_iota(jnp.int32, (rows, rows), 0)
    moves = (target == place).astype(jnp.bfloat16)
    out[...] = dot(moves, total.astype(jnp.bfloat16), NT).astype(jnp.bfloat16)


def sum_chips(parts, out):
    total = jnp.sum(parts[...].astype(jnp.float32), axis=0).astype(jnp.bfloat16)
    rows = out.shape[0] * out.shape[1]
    target = lax.broadcasted_iota(jnp.int32, (rows, 1), 0)
    place = jnp.where((target & 7) < 5, (target >> 3) * 5 + (target & 7), -1)
    source = lax.broadcasted_iota(jnp.int32, (rows, total.shape[0]), 1)
    moves = (source == place).astype(jnp.bfloat16)
    spread = dot(moves, total, (((1,), (0,)), ((), ())))
    out[...] = spread.astype(jnp.bfloat16).reshape(out.shape)


def sum_planes(parts, out):
    total = jnp.sum(parts[...].astype(jnp.float32).reshape(Z, C, 8, 256), axis=0)
    out[:, :256] = total[0, :5]
    out[:, 256:] = total[1, :5]


def input_product(*refs):
    grad, out = refs[0], refs[-1]
    z, core = lax.axis_index("zl"), lax.axis_index("c")
    for step in range(ZL):
        own, other = refs[1 + step][...], refs[1 + ZL + step][...]
        pair = jnp.where(core == 0, own, other), jnp.where(core == 0, other, own)
        rows = own.shape[0] // Y
        block = jnp.concatenate([half[y * rows : (y + 1) * rows] for y in range(Y) for half in pair], axis=0)
        columns = pl.ds(pl.multiple_of(((z + step) % ZL) * 640, 128), 640)
        out[:, columns] = dot(grad[...], block, NT).astype(jnp.bfloat16)


def params():
    return pltpu.CompilerParams(vmem_limit_bytes=VMEM_LIMIT)


def body(act, grad, weight):
    act_other = shift(act, "c", 1, C)
    grad_other = shift(grad, "c", 1, C)
    rows = act.shape[1] // X
    tokens = act.shape[0]
    partial = pl.pallas_call(
        pair_product,
        grid=(X,),
        in_specs=[pl.BlockSpec((tokens, rows), lambda i: (0, i))] * 2 + [pl.BlockSpec(grad.shape, lambda i: (0, 0))] * 2,
        out_specs=pl.BlockSpec((rows, 256), lambda i: (i, 0)),
        out_shape=jax.ShapeDtypeStruct((X * rows, 256), jnp.bfloat16),
        compiler_params=params(),
        name="pair_product",
    )(act, act_other, grad, grad_other)
    partial = partial.reshape(X * Y, rows // Y, 256)
    partial, weight = lax.optimization_barrier((partial, weight))
    parts = all_to_all(partial, ("x", "y"))

    own = lax.all_gather(weight, "y", axis=0, tiled=True)
    depth = own.shape[0]
    ring = ("zh", "zl")
    low = shift(own, ring, 1, Z)
    high = shift(own, ring, Z - 1, Z)
    far = (shift(own[: depth // 2], ring, 2, Z), shift(own[depth // 2 :], ring, Z - 2, Z))
    far = jnp.concatenate(far, axis=0)
    pieces = [own, high, far, low]
    others = [shift(p, "c", 1, C) for p in pieces]

    chip_sum = pl.pallas_call(
        sum_chips,
        out_shape=jax.ShapeDtypeStruct((Z * C, 8, 256), jnp.bfloat16),
        compiler_params=params(),
        name="sum_chips",
    )(parts)
    planes = all_to_all(chip_sum, ("zh", "zl", "c"))

    input_grad = pl.pallas_call(
        input_product,
        out_shape=jax.ShapeDtypeStruct(act.shape, jnp.bfloat16),
        compiler_params=params(),
        name="input_product",
    )(grad, *pieces, *others)
    weight_grad = pl.pallas_call(
        sum_planes,
        out_shape=jax.ShapeDtypeStruct((5, 512), jnp.float32),
        compiler_params=params(),
        name="sum_planes",
    )(planes)
    return input_grad, weight_grad


def solution(mesh):
    fine = Mesh(mesh.devices.reshape(X, ZH, ZL, Y, C), ("x", "zh", "zl", "y", "c"))
    every = P(("x", "zh", "zl", "y", "c"), None)
    return jax.shard_map(
        body,
        mesh=fine,
        in_specs=(every, every, P(("zl", "y", "c"), None)),
        out_specs=(every, every),
        check_vma=False,
    )
```

time: 212 us -> 96.4 us (0.45)
  the two profiles are of different devices: /device:TPU:1 before, /device:TPU:2 now
where the time goes in v1:
time: 96.4 us; the launch traced here: 95.8 us
  starting transfers between devices  49.8 us (52%)
  blocking collectives  25.4 us (26%)
  waiting for transfers between devices  9.89 us (10%)
  Pallas kernels  7.74 us (8%)
  local copies, waits for them, and re-layouts  2.19 us (2%)
    ppermute x10, starting transfers between devices, shift(): return lax.ppermute(a, axes, [(i, (i + step) % size) for i in range(size)])  30.9 us
    all_gather x1, blocking collectives, body(): own = lax.all_gather(weight, 'y', axis=0, tiled=True)  25.4 us
    all_to_all x2, starting transfers between devices, all_to_all(): return lax.all_to_all(a, axes, split_axis=0, concat_axis=0, tiled=True)  18.9 us
    all_to_all x2, waiting for transfers between devices, all_to_all(): return lax.all_to_all(a, axes, split_axis=0, concat_axis=0, tiled=True)  7.31 us
    pallas_call x1, Pallas kernels, body(): pl.pallas_call(pair_product, grid=(X,), in_specs=[pl.BlockSpec((tokens, r...  4.11 us
    ppermute x10, waiting for transfers between devices, shift(): return lax.ppermute(a, axes, [(i, (i + step) % size) for i in range(size)])  2.58 us
    unnamed x9, local copies, waits for them, and re-layouts  2.15 us
    pallas_call x1, Pallas kernels, body(): pl.pallas_call(input_product, out_shape=jax.ShapeDtypeStruct(act.shape, j...  1.96 us
  transfers between devices with their start and end apart: 12, of which 3 were waited for; matrix products, arithmetic and copies ran while one was open for 0% of the time, Pallas kernels for 3%

profile of v1, /device:TPU:2, one launch (start us, length us, event | category | flops | bytes accessed | tf_op | source)
XLA Modules:
  0.0 95.8 jit_solution(5726502679642567558)
XLA Ops:
  0.6 1.9 %collective-permute-start = (bf16[192,2560]{1,0:T(8,128)(2,1)}, bf16[192,2560]{1,0:T(8,128)(2,1)S(1)}, u32[]{:S(2)}, u32[]{:S(2)}) collective-permute-start(bf16[192,2560]{1,0:T(8,128)(2,1)} %act.1), channel_id=1, source_target_pairs={{0,1},{1,0},{2,3},{3,2},{4,5},{5,4},{6,7},{7,6},{8,9},{9,8},{10,11... | collective-permute-start | bytes 2949128 | tf_op jit(solution)/shard_map/ppermute | solution.py:25
  2.6 2.4 %collective-permute-start.1 = (bf16[192,512]{1,0:T(8,128)(2,1)}, bf16[192,512]{1,0:T(8,128)(2,1)S(1)}, u32[]{:S(2)}, u32[]{:S(2)}) collective-permute-start(bf16[192,512]{1,0:T(8,128)(2,1)} %refs_0_.1), channel_id=1, source_target_pairs={{0,1},{1,0},{2,3},{3,2},{4,5},{5,4},{6,7},{7,6},{8,9},{9,8},{10,11... | collective-permute-start | bytes 589832 | tf_op jit(solution)/shard_map/ppermute | solution.py:25
  5.0 1.3 %collective-permute-done.1.grad_other = bf16[192,512]{1,0:T(8,128)(2,1)S(1)} collective-permute-done((bf16[192,512]{1,0:T(8,128)(2,1)}, bf16[192,512]{1,0:T(8,128)(2,1)S(1)}, u32[]{:S(2)}, u32[]{:S(2)}) %collective-permute-start.1) | collective-permute-done | bytes 196640 | tf_op jit(solution)/shard_map/ppermute | solution.py:25
  6.2 0.0 collective-permute-done.act_other
  6.2 1.2 %copy-done = bf16[192,2560]{1,0:T(8,128)(2,1)S(1)} copy-done((bf16[192,2560]{1,0:T(8,128)(2,1)S(1)}, bf16[192,2560]{1,0:T(8,128)(2,1)}, u32[]{:S(2)}) %copy-start) | copy-done | bytes 983064
  7.4 0.9 copy-done.1
  8.4 4.1 %pair_product.1 = bf16[2560,256]{1,0:T(8,128)(2,1)} custom-call(bf16[192,2560]{1,0:T(8,128)(2,1)S(1)} %copy-done, bf16[192,2560]{1,0:T(8,128)(2,1)S(1)} %collective-permute-done.act_other, bf16[192,512]{1,0:T(8,128)(2,1)S(1)} %copy-done.1, bf16[192,512]{1,0:T(8,128)(2,1)S(1)} %collective-permute-done.1.grad_other), custom_call_target="tpu_custom_call" | custom-call | tf_op jit(solution)/shard_map/pair_product/pallas_call | solution.py:78
  12.5 9.5 %all-to-all-start = ((bf16[16,160,256]{2,1,0:T(8,128)(2,1)}), bf16[16,160,256]{2,1,0:T(8,128)(2,1)S(1)}, u32[]{:S(2)}, u32[]{:S(2)}) async-start(bf16[16,160,256]{2,1,0:T(8,128)(2,1)} %bitcast), calls=%async_computation | async-start | bytes 2621440 | tf_op jit(solution)/shard_map/all_to_all | solution.py:21
  22.0 25.4 %all_gather.3.refs_1_ = bf16[320,512]{1,0:T(8,128)(2,1)S(1)} all-gather(bf16[80,512]{1,0:T(8,128)(2,1)S(1)} %copy-done.3), channel_id=1, replica_groups=mesh['x'=4,'zh'=4,'zl'=4,'y'=4,'c'=2] {'y'}, dimensions={0}, use_global_device_ids=true | all-gather | bytes 409600 | tf_op jit(solution)/shard_map/all_gather | solution.py:91
  47.5 0.0 copy-start.2
  47.5 3.3 %collective-permute-start.3 = (bf16[160,512]{1,0:T(8,128)(2,1)S(1)}, bf16[160,512]{1,0:T(8,128)(2,1)S(1)}, u32[]{:S(2)}, u32[]{:S(2)}) collective-permute-start(bf16[160,512]{1,0:T(8,128)(2,1)S(1)} %get-tuple-element.7), channel_id=1, source_target_pairs={{0,16},{8,24},{16,32},{24,40},{32,48},{40,56},{48,64},{56,72},{64,... | collective-permute-start | bytes 491528 | tf_op jit(solution)/shard_map/ppermute | solution.py:25
  50.8 3.8 %collective-permute-start.5 = (bf16[320,512]{1,0:T(8,128)(2,1)S(1)}, bf16[320,512]{1,0:T(8,128)(2,1)S(1)}, u32[]{:S(2)}, u32[]{:S(2)}) collective-permute-start(bf16[320,512]{1,0:T(8,128)(2,1)S(1)} %all_gather.3.refs_1_), channel_id=1, source_target_pairs={{0,8},{8,16},{16,24},{24,32},{32,40},{40,48},{48,56},{56,64},{64,7... | collective-permute-start | bytes 983048 | tf_op jit(solution)/shard_map/ppermute | solution.py:25
  54.6 6.2 %collective-permute-start.2 = (bf16[320,512]{1,0:T(8,128)(2,1)S(1)}, bf16[320,512]{1,0:T(8,128)(2,1)S(1)}, u32[]{:S(2)}, u32[]{:S(2)}) collective-permute-start(bf16[320,512]{1,0:T(8,128)(2,1)S(1)} %all_gather.3.refs_1_), channel_id=1, source_target_pairs={{0,120},{8,0},{16,8},{24,16},{32,24},{40,32},{48,40},{56,48},{64,5... | collective-permute-start | bytes 983048 | tf_op jit(solution)/shard_map/ppermute | solution.py:25
  60.9 4.8 %collective-permute-start.4 = (bf16[160,512]{1,0:T(8,128)(2,1)S(1)}, bf16[160,512]{1,0:T(8,128)(2,1)S(1)}, u32[]{:S(2)}, u32[]{:S(2)}) collective-permute-start(bf16[160,512]{1,0:T(8,128)(2,1)S(1)} %get-tuple-element.6), channel_id=1, source_target_pairs={{0,112},{8,120},{16,0},{24,8},{32,16},{40,24},{48,32},{56,40},{64,... | collective-permute-start | bytes 491528 | tf_op jit(solution)/shard_map/ppermute | solution.py:25
  65.7 1.9 %collective-permute-start.6 = (bf16[320,512]{1,0:T(8,128)(2,1)S(1)}, bf16[320,512]{1,0:T(8,128)(2,1)S(1)}, u32[]{:S(2)}, u32[]{:S(2)}) collective-permute-start(bf16[320,512]{1,0:T(8,128)(2,1)S(1)} %all_gather.3.refs_1_), channel_id=1, source_target_pairs={{0,1},{1,0},{2,3},{3,2},{4,5},{5,4},{6,7},{7,6},{8,9},{9,8},{10,11... | collective-permute-start | bytes 983048 | tf_op jit(solution)/shard_map/ppermute | solution.py:25
  67.6 0.0 all-to-all-done.parts
  67.6 1.0 %sum_chips.1 = bf16[32,8,256]{2,1,0:T(8,128)(2,1)} custom-call(bf16[16,160,256]{2,1,0:T(8,128)(2,1)S(1)} %all-to-all-done.parts), custom_call_target="tpu_custom_call" | custom-call | tf_op jit(solution)/shard_map/sum_chips/pallas_call | solution.py:101
  68.7 9.3 %all-to-all-start.1 = ((bf16[32,8,256]{2,1,0:T(8,128)(2,1)}), bf16[32,8,256]{2,1,0:T(8,128)(2,1)S(1)}, u32[]{:S(2)}, u32[]{:S(2)}) async-start(bf16[32,8,256]{2,1,0:T(8,128)(2,1)} %sum_chips.1), calls=%async_computation.1 | async-start | bytes 262144 | tf_op jit(solution)/shard_map/all_to_all | solution.py:21
  78.0 0.0 collective-permute-done.3
  78.0 0.0 collective-permute-done.4
  78.0 2.2 %collective-permute-start.8 = (bf16[320,512]{1,0:T(8,128)(2,1)S(1)}, bf16[320,512]{1,0:T(8,128)(2,1)S(1)}, u32[]{:S(2)}, u32[]{:S(2)}) collective-permute-start(bf16[320,512]{1,0:T(8,128)(2,1)S(1)} %constant_dynamic-update-slice_fusion.refs_3_), channel_id=1, source_target_pairs={{0,1},{1,0},{2,3},{3,2},{4,5},{5,4},{6,7},{7,6},{8,9},{9,8},{10,11... | collective-permute-start | bytes 983048 | tf_op jit(solution)/shard_map/ppermute | solution.py:25
  80.2 0.0 collective-permute-done.5.refs_4_
  80.2 2.1 %collective-permute-start.9 = (bf16[320,512]{1,0:T(8,128)(2,1)S(1)}, bf16[320,512]{1,0:T(8,128)(2,1)S(1)}, u32[]{:S(2)}, u32[]{:S(2)}) collective-permute-start(bf16[320,512]{1,0:T(8,128)(2,1)S(1)} %collective-permute-done.5.refs_4_), channel_id=1, source_target_pairs={{0,1},{1,0},{2,3},{3,2},{4,5},{5,4},{6,7},{7,6},{8,9},{9,8},{10,11... | collective-permute-start | bytes 983048 | tf_op jit(solution)/shard_map/ppermute | solution.py:25
  82.4 0.0 collective-permute-done.2.refs_2_
  82.4 2.2 %collective-permute-start.7 = (bf16[320,512]{1,0:T(8,128)(2,1)S(1)}, bf16[320,512]{1,0:T(8,128)(2,1)S(1)}, u32[]{:S(2)}, u32[]{:S(2)}) collective-permute-start(bf16[320,512]{1,0:T(8,128)(2,1)S(1)} %collective-permute-done.2.refs_2_), channel_id=1, source_target_pairs={{0,1},{1,0},{2,3},{3,2},{4,5},{5,4},{6,7},{7,6},{8,9},{9,8},{10,11... | collective-permute-start | bytes 983048 | tf_op jit(solution)/shard_map/ppermute | solution.py:25
  84.6 0.0 collective-permute-done.6.refs_5_
  84.6 0.0 collective-permute-done.8.refs_7_
  84.6 0.0 collective-permute-done.9.refs_8_
  84.6 1.3 %collective-permute-done.7.refs_6_ = bf16[320,512]{1,0:T(8,128)(2,1)S(1)} collective-permute-done((bf16[320,512]{1,0:T(8,128)(2,1)S(1)}, bf16[320,512]{1,0:T(8,128)(2,1)S(1)}, u32[]{:S(2)}, u32[]{:S(2)}) %collective-permute-start.7) | collective-permute-done | bytes 327712 | tf_op jit(solution)/shard_map/ppermute | solution.py:25
  85.9 2.0 %input_product.1 = bf16[192,2560]{1,0:T(8,128)(2,1)} custom-call(bf16[192,512]{1,0:T(8,128)(2,1)S(1)} %copy-done.2, bf16[320,512]{1,0:T(8,128)(2,1)S(1)} %all_gather.3.refs_1_, bf16[320,512]{1,0:T(8,128)(2,1)S(1)} %collective-permute-done.2.refs_2_, bf16[320,512]{1,0:T(8,128)(2,1)S(1)} %constant_dynamic-update-slice_fusion.refs_3_, ...), custom_call_target="tpu_custom_call" | custom-call | tf_op jit(solution)/shard_map/input_product/pallas_call | solution.py:109
  87.9 7.3 %all-to-all-done.1.parts = bf16[32,8,256]{2,1,0:T(8,128)(2,1)S(1)} async-done(((bf16[32,8,256]{2,1,0:T(8,128)(2,1)}), bf16[32,8,256]{2,1,0:T(8,128)(2,1)S(1)}, u32[]{:S(2)}, u32[]{:S(2)}) %all-to-all-start.1) | async-done | bytes 131104 | tf_op jit(solution)/shard_map/all_to_all | solution.py:21
  95.2 0.6 sum_planes.1
  (8 shorter events, 0.1 us)
Async XLA Ops:
  0.6 5.6 %collective-permute-start = (bf16[192,2560]{1,0:T(8,128)(2,1)}, bf16[192,2560]{1,0:T(8,128)(2,1)S(1)}, u32[]{:S(2)}, u32[]{:S(2)}) collective-permute-start(bf16[192,2560]{1,0:T(8,128)(2,1)} %act.1), channel_id=1, source_target_pairs={{0,1},{1,0},{2,3},{3,2},{4,5},{5,4},{6,7},{7,6},{8,9},{9,8},{10,11... | collective-permute-start | bytes 2949128 | tf_op jit(solution)/shard_map/ppermute | solution.py:25
  2.6 3.7 %collective-permute-start.1 = (bf16[192,512]{1,0:T(8,128)(2,1)}, bf16[192,512]{1,0:T(8,128)(2,1)S(1)}, u32[]{:S(2)}, u32[]{:S(2)}) collective-permute-start(bf16[192,512]{1,0:T(8,128)(2,1)} %refs_0_.1), channel_id=1, source_target_pairs={{0,1},{1,0},{2,3},{3,2},{4,5},{5,4},{6,7},{7,6},{8,9},{9,8},{10,11... | collective-permute-start | bytes 589832 | tf_op jit(solution)/shard_map/ppermute | solution.py:25
  6.2 1.2 %copy-start = (bf16[192,2560]{1,0:T(8,128)(2,1)S(1)}, bf16[192,2560]{1,0:T(8,128)(2,1)}, u32[]{:S(2)}) copy-start(bf16[192,2560]{1,0:T(8,128)(2,1)} %act.1) | copy-start | bytes 2949124
  7.4 0.9 copy-start.1
  12.5 9.6 %copy-start.3 = (bf16[80,512]{1,0:T(8,128)(2,1)S(1)}, bf16[80,512]{1,0:T(8,128)(2,1)}, u32[]{:S(2)}) copy-start(bf16[80,512]{1,0:T(8,128)(2,1)} %param.5) | copy-start | bytes 245764
  12.5 55.1 %all-to-all-start = ((bf16[16,160,256]{2,1,0:T(8,128)(2,1)}), bf16[16,160,256]{2,1,0:T(8,128)(2,1)S(1)}, u32[]{:S(2)}, u32[]{:S(2)}) async-start(bf16[16,160,256]{2,1,0:T(8,128)(2,1)} %bitcast), calls=%async_computation | async-start | bytes 2621440 | tf_op jit(solution)/shard_map/all_to_all | solution.py:21
  47.5 38.5 %copy-start.2 = (bf16[192,512]{1,0:T(8,128)(2,1)S(1)}, bf16[192,512]{1,0:T(8,128)(2,1)}, u32[]{:S(2)}) copy-start(bf16[192,512]{1,0:T(8,128)(2,1)} %refs_0_.1) | copy-start | bytes 589828
  47.5 30.5 %collective-permute-start.3 = (bf16[160,512]{1,0:T(8,128)(2,1)S(1)}, bf16[160,512]{1,0:T(8,128)(2,1)S(1)}, u32[]{:S(2)}, u32[]{:S(2)}) collective-permute-start(bf16[160,512]{1,0:T(8,128)(2,1)S(1)} %get-tuple-element.7), channel_id=1, source_target_pairs={{0,16},{8,24},{16,32},{24,40},{32,48},{40,56},{48,64},{56,72},{64,... | collective-permute-start | bytes 491528 | tf_op jit(solution)/shard_map/ppermute | solution.py:25
  50.8 29.5 %collective-permute-start.5 = (bf16[320,512]{1,0:T(8,128)(2,1)S(1)}, bf16[320,512]{1,0:T(8,128)(2,1)S(1)}, u32[]{:S(2)}, u32[]{:S(2)}) collective-permute-start(bf16[320,512]{1,0:T(8,128)(2,1)S(1)} %all_gather.3.refs_1_), channel_id=1, source_target_pairs={{0,8},{8,16},{16,24},{24,32},{32,40},{40,48},{48,56},{56,64},{64,7... | collective-permute-start | bytes 983048 | tf_op jit(solution)/shard_map/ppermute | solution.py:25
  54.6 27.8 %collective-permute-start.2 = (bf16[320,512]{1,0:T(8,128)(2,1)S(1)}, bf16[320,512]{1,0:T(8,128)(2,1)S(1)}, u32[]{:S(2)}, u32[]{:S(2)}) collective-permute-start(bf16[320,512]{1,0:T(8,128)(2,1)S(1)} %all_gather.3.refs_1_), channel_id=1, source_target_pairs={{0,120},{8,0},{16,8},{24,16},{32,24},{40,32},{48,40},{56,48},{64,5... | collective-permute-start | bytes 983048 | tf_op jit(solution)/shard_map/ppermute | solution.py:25
  60.9 17.2 %collective-permute-start.4 = (bf16[160,512]{1,0:T(8,128)(2,1)S(1)}, bf16[160,512]{1,0:T(8,128)(2,1)S(1)}, u32[]{:S(2)}, u32[]{:S(2)}) collective-permute-start(bf16[160,512]{1,0:T(8,128)(2,1)S(1)} %get-tuple-element.6), channel_id=1, source_target_pairs={{0,112},{8,120},{16,0},{24,8},{32,16},{40,24},{48,32},{56,40},{64,... | collective-permute-start | bytes 491528 | tf_op jit(solution)/shard_map/ppermute | solution.py:25
  65.7 18.9 %collective-permute-start.6 = (bf16[320,512]{1,0:T(8,128)(2,1)S(1)}, bf16[320,512]{1,0:T(8,128)(2,1)S(1)}, u32[]{:S(2)}, u32[]{:S(2)}) collective-permute-start(bf16[320,512]{1,0:T(8,128)(2,1)S(1)} %all_gather.3.refs_1_), channel_id=1, source_target_pairs={{0,1},{1,0},{2,3},{3,2},{4,5},{5,4},{6,7},{7,6},{8,9},{9,8},{10,11... | collective-permute-start | bytes 983048 | tf_op jit(solution)/shard_map/ppermute | solution.py:25
  68.7 26.5 %all-to-all-start.1 = ((bf16[32,8,256]{2,1,0:T(8,128)(2,1)}), bf16[32,8,256]{2,1,0:T(8,128)(2,1)S(1)}, u32[]{:S(2)}, u32[]{:S(2)}) async-start(bf16[32,8,256]{2,1,0:T(8,128)(2,1)} %sum_chips.1), calls=%async_computation.1 | async-start | bytes 262144 | tf_op jit(solution)/shard_map/all_to_all | solution.py:21
  78.0 6.6 %collective-permute-start.8 = (bf16[320,512]{1,0:T(8,128)(2,1)S(1)}, bf16[320,512]{1,0:T(8,128)(2,1)S(1)}, u32[]{:S(2)}, u32[]{:S(2)}) collective-permute-start(bf16[320,512]{1,0:T(8,128)(2,1)S(1)} %constant_dynamic-update-slice_fusion.refs_3_), channel_id=1, source_target_pairs={{0,1},{1,0},{2,3},{3,2},{4,5},{5,4},{6,7},{7,6},{8,9},{9,8},{10,11... | collective-permute-start | bytes 983048 | tf_op jit(solution)/shard_map/ppermute | solution.py:25
  80.2 4.4 %collective-permute-start.9 = (bf16[320,512]{1,0:T(8,128)(2,1)S(1)}, bf16[320,512]{1,0:T(8,128)(2,1)S(1)}, u32[]{:S(2)}, u32[]{:S(2)}) collective-permute-start(bf16[320,512]{1,0:T(8,128)(2,1)S(1)} %collective-permute-done.5.refs_4_), channel_id=1, source_target_pairs={{0,1},{1,0},{2,3},{3,2},{4,5},{5,4},{6,7},{7,6},{8,9},{9,8},{10,11... | collective-permute-start | bytes 983048 | tf_op jit(solution)/shard_map/ppermute | solution.py:25
  82.4 3.5 %collective-permute-start.7 = (bf16[320,512]{1,0:T(8,128)(2,1)S(1)}, bf16[320,512]{1,0:T(8,128)(2,1)S(1)}, u32[]{:S(2)}, u32[]{:S(2)}) collective-permute-start(bf16[320,512]{1,0:T(8,128)(2,1)S(1)} %collective-permute-done.2.refs_2_), channel_id=1, source_target_pairs={{0,1},{1,0},{2,3},{3,2},{4,5},{5,4},{6,7},{7,6},{8,9},{9,8},{10,11... | collective-permute-start | bytes 983048 | tf_op jit(solution)/shard_map/ppermute | solution.py:25

commit v2 on v1

v2 whole, which is shorter than its diff:
```python
import jax
import jax.numpy as jnp
from jax import lax
from jax.experimental import pallas as pl
from jax.experimental.pallas import tpu as pltpu
from jax.sharding import Mesh, PartitionSpec as P

X, ZH, ZL, Y, C = 4, 4, 4, 4, 2
Z = ZH * ZL
VMEM_LIMIT = 48 * 1024 * 1024

NT = (((1,), (1,)), ((), ()))
TN = (((0,), (0,)), ((), ()))


def dot(a, b, dims):
    return lax.dot_general(a, b, dims, preferred_element_type=jnp.float32)


def all_to_all(a, axes):
    return lax.all_to_all(a, axes, split_axis=0, concat_axis=0, tiled=True)


def shift(a, axes, step, size):
    return lax.ppermute(a, axes, [(i, (i + step) % size) for i in range(size)])


def pair_product(own, other, out, total):
    depth = own.shape[1] - 512
    half = pl.ds(pl.multiple_of(depth + lax.axis_index("c") * 256, 128), 256)
    rows = depth // X
    for x in range(X):
        columns = slice(x * rows, (x + 1) * rows)
        product = dot(own[:, columns], own[:, half], TN) + dot(other[:, columns], other[:, half], TN)
        for lane in range(2):
            lanes = slice(lane * 128, (lane + 1) * 128)
            total[x, lane] = product[:, lanes]
            for row in range(10 * Y):
                at = slice(x * rows + row * Z, x * rows + (row + 1) * Z)
                out[at, lanes] = total[x, lane, pl.ds(row, Z, stride=10 * Y), :].astype(jnp.bfloat16)


def sum_chips(parts, out, total):
    rows = parts.shape[1]
    summed = jnp.sum(parts[...].astype(jnp.float32), axis=0)
    for lane in range(2):
        lanes = slice(lane * 128, (lane + 1) * 128)
        total[lane, :rows] = summed[:, lanes]
        total[lane, rows:] = jnp.zeros((total.shape[1] - rows, 128), jnp.float32)
        for z in range(Z):
            for core in range(C):
                out[z * C + core, :, lanes] = total[lane, pl.ds(core * 5 * Z + z, 8, stride=Z), :].astype(jnp.bfloat16)


def sum_planes(parts, after, out):
    total = jnp.sum(parts[...].astype(jnp.float32).reshape(Z, C, 8, 256), axis=0)
    out[:, :256] = total[0, :5]
    out[:, 256:] = total[1, :5]


def input_product(*refs):
    grad, out, done = refs[0], refs[-2], refs[-1]
    me, z, core = lax.axis_index("y"), lax.axis_index("zl"), lax.axis_index("c")
    for step in range(ZL):
        own, other = refs[1 + step], refs[1 + ZL + step]
        block = []
        for y in range(Y):
            at = (y - me + Y) % Y
            pair = own[at], other[at]
            block += [jnp.where(core == 0, *pair), jnp.where(core == 0, *pair[::-1])]
        columns = pl.ds(pl.multiple_of(((z + step) % ZL) * 640, 128), 640)
        out[:, columns] = dot(grad[...], jnp.concatenate(block, axis=0), NT).astype(jnp.bfloat16)
    done[...] = jnp.zeros(done.shape, done.dtype)


def params(limit=VMEM_LIMIT):
    return pltpu.CompilerParams(vmem_limit_bytes=limit)


def join(pieces, after):
    def stack(*refs):
        for i in range(len(pieces)):
            refs[-1][i] = refs[i][...]

    return pl.pallas_call(
        stack,
        in_specs=[pl.BlockSpec(memory_space=pltpu.VMEM)] * len(pieces) + [pl.BlockSpec(memory_space=pl.ANY)],
        out_shape=jax.ShapeDtypeStruct((len(pieces),) + pieces[0].shape, pieces[0].dtype),
        compiler_params=params(),
        cost_estimate=pl.CostEstimate(flops=20_000_000_000, bytes_accessed=50_000_000, transcendentals=0),
        name="join",
    )(*pieces, after)


def body(act, grad, weight):
    column = [weight, shift(weight, "y", Y - 1, Y), shift(weight, "y", 2, Y), shift(weight, "y", 1, Y)]
    packed = jnp.concatenate([act, grad], axis=1)
    packed_other = shift(packed, "c", 1, C)
    rows = act.shape[1] // X
    partial = pl.pallas_call(
        pair_product,
        out_shape=jax.ShapeDtypeStruct((X * rows, 256), jnp.bfloat16),
        scratch_shapes=[pltpu.VMEM((X, 2, rows, 128), jnp.float32)],
        compiler_params=params(),
        name="pair_product",
    )(packed, packed_other)
    partial = partial.reshape(X * Y, rows // Y, 256)
    parts = all_to_all(partial, ("x", "y"))
    column = join(column, partial)

    ring = ("zh", "zl")
    across = [(((z + 2 - 4 * c) % Z) * C + c, z * C + c) for z in range(Z) for c in range(C)]
    far = lax.ppermute(column, ring + ("c",), across)
    own = [column, shift(column, ring, Z - 1, Z), far, shift(column, ring, 1, Z)]

    chip_sum = pl.pallas_call(
        sum_chips,
        out_shape=jax.ShapeDtypeStruct((Z * C, 8, 256), jnp.bfloat16),
        scratch_shapes=[pltpu.VMEM((2, 208, 128), jnp.float32)],
        compiler_params=params(),
        name="sum_chips",
    )(parts)
    planes = all_to_all(chip_sum, ("zh", "zl", "c"))
    other = [shift(piece, "c", 1, C) for piece in own]

    input_grad, done = pl.pallas_call(
        input_product,
        out_shape=(jax.ShapeDtypeStruct(act.shape, jnp.bfloat16), jax.ShapeDtypeStruct((8, 128), jnp.float32)),
        compiler_params=params(),
        name="input_product",
    )(grad, *own, *other)
    weight_grad = pl.pallas_call(
        sum_planes,
        in_specs=[pl.BlockSpec(memory_space=pltpu.VMEM), pl.BlockSpec(memory_space=pl.ANY)],
        out_shape=jax.ShapeDtypeStruct((5, 512), jnp.float32),
        compiler_params=params(),
        name="sum_planes",
    )(planes, done)
    return input_grad, weight_grad


def solution(mesh):
    fine = Mesh(mesh.devices.reshape(X, ZH, ZL, Y, C), ("x", "zh", "zl", "y", "c"))
    every = P(("x", "zh", "zl", "y", "c"), None)
    return jax.shard_map(
        body,
        mesh=fine,
        in_specs=(every, every, P(("zl", "y", "c"), None)),
        out_specs=(every, every),
        check_vma=False,
    )
```

time: 96.4 us -> 78.9 us (0.82)
  the two profiles are of different devices: /device:TPU:2 before, /device:TPU:1 now
where the time goes in v2:
time: 78.9 us; the launch traced here: 78.4 us
  starting transfers between devices  61 us (77%)
  waiting for transfers between devices  9.17 us (12%)
  Pallas kernels  6 us (8%)
  local copies, waits for them, and re-layouts  1.38 us (2%)
  between operations  0.87 us (1%)
    ppermute x10, starting transfers between devices, shift(): return lax.ppermute(a, axes, [(i, (i + step) % size) for i in range(size)])  33.7 us
    all_to_all x2, starting transfers between devices, all_to_all(): return lax.all_to_all(a, axes, split_axis=0, concat_axis=0, tiled=True)  22.3 us
    all_to_all x2, waiting for transfers between devices, all_to_all(): return lax.all_to_all(a, axes, split_axis=0, concat_axis=0, tiled=True)  7.84 us
    ppermute x1, starting transfers between devices, body(): far = lax.ppermute(column, ring + ('c',), across)  4.9 us
    pallas_call x1, Pallas kernels, body(): pl.pallas_call(pair_product, out_shape=jax.ShapeDtypeStruct((X * rows, 25...  2.47 us
    pallas_call x1, Pallas kernels, body(): pl.pallas_call(input_product, out_shape=(jax.ShapeDtypeStruct(act.shape,...  1.91 us
  transfers between devices with their start and end apart: 13, of which 3 were waited for; matrix products, arithmetic and copies ran while one was open for 0% of the time, Pallas kernels for 7%

profile of v2, /device:TPU:1, one launch (start us, length us, event | category | flops | bytes accessed | tf_op | source)
XLA Modules:
  0.0 78.4 jit_solution(11233128727615824798)
XLA Ops:
  0.6 0.0 copy-start
  0.6 1.4 %constant_dynamic-update-slice_fusion.1 = bf16[192,3072]{1,0:T(8,128)(2,1)S(1)} fusion(bf16[192,2560]{1,0:T(8,128)(2,1)} %param.3), kind=kLoop, calls=%fused_computation.1 | loop fusion | bytes 1966080
  2.0 8.8 %collective-permute-start.3 = (bf16[192,3072]{1,0:T(8,128)(2,1)S(1)}, bf16[192,3072]{1,0:T(8,128)(2,1)S(1)}, u32[]{:S(2)}, u32[]{:S(2)}) collective-permute-start(bf16[192,3072]{1,0:T(8,128)(2,1)S(1)} %constant_dynamic-update-slice_fusion.own), channel_id=1, source_target_pairs={{0,1},{1,0},{2,3},{3,2},{4,5},{5,4},{6,7},{7,6},{8,9},{9,8},{10,11... | collective-permute-start | bytes 3538952 | tf_op jit(solution)/shard_map/ppermute | solution.py:25
  10.8 1.9 %collective-permute-start.1 = (bf16[80,512]{1,0:T(8,128)(2,1)S(1)}, bf16[80,512]{1,0:T(8,128)(2,1)S(1)}, u32[]{:S(2)}, u32[]{:S(2)}) collective-permute-start(bf16[80,512]{1,0:T(8,128)(2,1)S(1)} %copy-done.1), channel_id=1, source_target_pairs={{0,4},{2,6},{4,0},{6,2},{1,5},{3,7},{5,1},{7,3},{8,12},{10,14},{12... | collective-permute-start | bytes 245768 | tf_op jit(solution)/shard_map/ppermute | solution.py:25
  12.8 1.9 %collective-permute-start = (bf16[80,512]{1,0:T(8,128)(2,1)S(1)}, bf16[80,512]{1,0:T(8,128)(2,1)S(1)}, u32[]{:S(2)}, u32[]{:S(2)}) collective-permute-start(bf16[80,512]{1,0:T(8,128)(2,1)S(1)} %copy-done.1), channel_id=1, source_target_pairs={{0,6},{2,0},{4,2},{6,4},{1,7},{3,1},{5,3},{7,5},{8,14},{10,8},{12,... | collective-permute-start | bytes 245768 | tf_op jit(solution)/shard_map/ppermute | solution.py:25
  14.7 3.4 %collective-permute-start.2 = (bf16[80,512]{1,0:T(8,128)(2,1)S(1)}, bf16[80,512]{1,0:T(8,128)(2,1)S(1)}, u32[]{:S(2)}, u32[]{:S(2)}) collective-permute-start(bf16[80,512]{1,0:T(8,128)(2,1)S(1)} %copy-done.1), channel_id=1, source_target_pairs={{0,2},{2,4},{4,6},{6,0},{1,3},{3,5},{5,7},{7,1},{8,10},{10,12},{12... | collective-permute-start | bytes 245768 | tf_op jit(solution)/shard_map/ppermute | solution.py:25
  18.1 0.0 collective-permute-done.3.other
  18.1 2.5 %pair_product.1 = bf16[2560,256]{1,0:T(8,128)(2,1)} custom-call(bf16[192,3072]{1,0:T(8,128)(2,1)S(1)} %constant_dynamic-update-slice_fusion.own, bf16[192,3072]{1,0:T(8,128)(2,1)S(1)} %collective-permute-done.3.other), custom_call_target="tpu_custom_call" | custom-call | tf_op jit(solution)/shard_map/pair_product/pallas_call | solution.py:100
  20.6 4.3 %all-to-all-start = ((bf16[16,160,256]{2,1,0:T(8,128)(2,1)}), bf16[16,160,256]{2,1,0:T(8,128)(2,1)S(1)}, u32[]{:S(2)}, u32[]{:S(2)}) async-start(bf16[16,160,256]{2,1,0:T(8,128)(2,1)} %bitcast.refs_4_), calls=%async_computation | async-start | bytes 2621440 | tf_op jit(solution)/shard_map/all_to_all | solution.py:21
  24.9 0.0 collective-permute-done.1.refs_2_
  24.9 0.0 collective-permute-done.refs_1_
  24.9 0.0 collective-permute-done.2.refs_3_
  25.0 2.6 %collective-permute-start.6 = (bf16[4,80,512]{2,1,0:T(8,128)(2,1)S(1)}, bf16[4,80,512]{2,1,0:T(8,128)(2,1)S(1)}, u32[]{:S(2)}, u32[]{:S(2)}) collective-permute-start(bf16[4,80,512]{2,1,0:T(8,128)(2,1)S(1)} %join.1.refs_1_), channel_id=1, source_target_pairs={{0,8},{8,16},{16,24},{24,32},{32,40},{40,48},{48,56},{56,64},{64,7... | collective-permute-start | bytes 983048 | tf_op jit(solution)/shard_map/ppermute | solution.py:25
  27.5 4.9 %collective-permute-start.5 = (bf16[4,80,512]{2,1,0:T(8,128)(2,1)S(1)}, bf16[4,80,512]{2,1,0:T(8,128)(2,1)S(1)}, u32[]{:S(2)}, u32[]{:S(2)}) collective-permute-start(bf16[4,80,512]{2,1,0:T(8,128)(2,1)S(1)} %join.1.refs_1_), channel_id=1, source_target_pairs={{16,0},{113,1},{24,8},{121,9},{32,16},{1,17},{40,24},{9,25},{48,32... | collective-permute-start | bytes 983048 | tf_op jit(solution)/shard_map/ppermute | solution.py:113
  32.4 6.5 %collective-permute-start.4 = (bf16[4,80,512]{2,1,0:T(8,128)(2,1)S(1)}, bf16[4,80,512]{2,1,0:T(8,128)(2,1)S(1)}, u32[]{:S(2)}, u32[]{:S(2)}) collective-permute-start(bf16[4,80,512]{2,1,0:T(8,128)(2,1)S(1)} %join.1.refs_1_), channel_id=1, source_target_pairs={{0,120},{8,0},{16,8},{24,16},{32,24},{40,32},{48,40},{56,48},{64,5... | collective-permute-start | bytes 983048 | tf_op jit(solution)/shard_map/ppermute | solution.py:25
  39.0 4.0 %all-to-all-done.parts = bf16[16,160,256]{2,1,0:T(8,128)(2,1)S(1)} async-done(((bf16[16,160,256]{2,1,0:T(8,128)(2,1)}), bf16[16,160,256]{2,1,0:T(8,128)(2,1)S(1)}, u32[]{:S(2)}, u32[]{:S(2)}) %all-to-all-start) | async-done | bytes 1310752 | tf_op jit(solution)/shard_map/all_to_all | solution.py:21
  42.9 1.0 %sum_chips.1 = bf16[32,8,256]{2,1,0:T(8,128)(2,1)} custom-call(bf16[16,160,256]{2,1,0:T(8,128)(2,1)S(1)} %all-to-all-done.parts), custom_call_target="tpu_custom_call" | custom-call | tf_op jit(solution)/shard_map/sum_chips/pallas_call | solution.py:116
  43.9 18.0 %all-to-all-start.1 = ((bf16[32,8,256]{2,1,0:T(8,128)(2,1)}), bf16[32,8,256]{2,1,0:T(8,128)(2,1)S(1)}, u32[]{:S(2)}, u32[]{:S(2)}) async-start(bf16[32,8,256]{2,1,0:T(8,128)(2,1)} %sum_chips.1), calls=%async_computation.1 | async-start | bytes 262144 | tf_op jit(solution)/shard_map/all_to_all | solution.py:21
  61.9 2.1 %collective-permute-start.7 = (bf16[4,80,512]{2,1,0:T(8,128)(2,1)S(1)}, bf16[4,80,512]{2,1,0:T(8,128)(2,1)S(1)}, u32[]{:S(2)}, u32[]{:S(2)}) collective-permute-start(bf16[4,80,512]{2,1,0:T(8,128)(2,1)S(1)} %join.1.refs_1_), channel_id=1, source_target_pairs={{0,1},{1,0},{2,3},{3,2},{4,5},{5,4},{6,7},{7,6},{8,9},{9,8},{10,11... | collective-permute-start | bytes 983048 | tf_op jit(solution)/shard_map/ppermute | solution.py:25
  64.0 0.0 collective-permute-done.6.refs_4_
  64.1 2.2 %collective-permute-start.10 = (bf16[4,80,512]{2,1,0:T(8,128)(2,1)S(1)}, bf16[4,80,512]{2,1,0:T(8,128)(2,1)S(1)}, u32[]{:S(2)}, u32[]{:S(2)}) collective-permute-start(bf16[4,80,512]{2,1,0:T(8,128)(2,1)S(1)} %collective-permute-done.6.refs_4_), channel_id=1, source_target_pairs={{0,1},{1,0},{2,3},{3,2},{4,5},{5,4},{6,7},{7,6},{8,9},{9,8},{10,11... | collective-permute-start | bytes 983048 | tf_op jit(solution)/shard_map/ppermute | solution.py:25
  66.2 0.0 collective-permute-done.5.refs_3_
  66.3 2.1 %collective-permute-start.9 = (bf16[4,80,512]{2,1,0:T(8,128)(2,1)S(1)}, bf16[4,80,512]{2,1,0:T(8,128)(2,1)S(1)}, u32[]{:S(2)}, u32[]{:S(2)}) collective-permute-start(bf16[4,80,512]{2,1,0:T(8,128)(2,1)S(1)} %collective-permute-done.5.refs_3_), channel_id=1, source_target_pairs={{0,1},{1,0},{2,3},{3,2},{4,5},{5,4},{6,7},{7,6},{8,9},{9,8},{10,11... | collective-permute-start | bytes 983048 | tf_op jit(solution)/shard_map/ppermute | solution.py:25
  68.4 0.0 collective-permute-done.4.refs_2_
  68.4 2.2 %collective-permute-start.8 = (bf16[4,80,512]{2,1,0:T(8,128)(2,1)S(1)}, bf16[4,80,512]{2,1,0:T(8,128)(2,1)S(1)}, u32[]{:S(2)}, u32[]{:S(2)}) collective-permute-start(bf16[4,80,512]{2,1,0:T(8,128)(2,1)S(1)} %collective-permute-done.4.refs_2_), channel_id=1, source_target_pairs={{0,1},{1,0},{2,3},{3,2},{4,5},{5,4},{6,7},{7,6},{8,9},{9,8},{10,11... | collective-permute-start | bytes 983048 | tf_op jit(solution)/shard_map/ppermute | solution.py:25
  70.6 0.0 collective-permute-done.7.refs_5_
  70.6 0.0 collective-permute-done.10.refs_8_
  70.6 0.0 collective-permute-done.9.refs_7_
  70.6 1.3 %collective-permute-done.8.refs_6_ = bf16[4,80,512]{2,1,0:T(8,128)(2,1)S(1)} collective-permute-done((bf16[4,80,512]{2,1,0:T(8,128)(2,1)S(1)}, bf16[4,80,512]{2,1,0:T(8,128)(2,1)S(1)}, u32[]{:S(2)}, u32[]{:S(2)}) %collective-permute-start.8) | collective-permute-done | bytes 327712 | tf_op jit(solution)/shard_map/ppermute | solution.py:25
  71.9 1.9 %input_product.1 = (bf16[192,2560]{1,0:T(8,128)(2,1)}, f32[8,128]{1,0:T(8,128)S(1)}) custom-call(bf16[192,512]{1,0:T(8,128)(2,1)S(1)} %copy-done, bf16[4,80,512]{2,1,0:T(8,128)(2,1)S(1)} %join.1.refs_1_, bf16[4,80,512]{2,1,0:T(8,128)(2,1)S(1)} %collective-permute-done.4.refs_2_, bf16[4,80,512]{2,1,0:T(8,128)(2,1)S(1)} %collective-permute-done.5.refs_3_, ...), custom_call_target="tpu_custom_call" | custom-call | tf_op jit(solution)/shard_map/input_product/pallas_call | solution.py:126
  73.9 3.9 %all-to-all-done.1.parts = bf16[32,8,256]{2,1,0:T(8,128)(2,1)S(1)} async-done(((bf16[32,8,256]{2,1,0:T(8,128)(2,1)}), bf16[32,8,256]{2,1,0:T(8,128)(2,1)S(1)}, u32[]{:S(2)}, u32[]{:S(2)}) %all-to-all-start.1) | async-done | bytes 131104 | tf_op jit(solution)/shard_map/all_to_all | solution.py:21
  77.7 0.6 sum_planes.1
  (5 shorter events, 0.0 us)
Async XLA Ops:
  0.6 1.4 %copy-start = (bf16[192,512]{1,0:T(8,128)(2,1)S(1)}, bf16[192,512]{1,0:T(8,128)(2,1)}, u32[]{:S(2)}) copy-start(bf16[192,512]{1,0:T(8,128)(2,1)} %refs_0_.3) | copy-start | bytes 589828
  0.6 10.2 %copy-start.1 = (bf16[80,512]{1,0:T(8,128)(2,1)S(1)}, bf16[80,512]{1,0:T(8,128)(2,1)}, u32[]{:S(2)}) copy-start(bf16[80,512]{1,0:T(8,128)(2,1)} %refs_0_.2) | copy-start | bytes 245764
  2.0 16.0 %collective-permute-start.3 = (bf16[192,3072]{1,0:T(8,128)(2,1)S(1)}, bf16[192,3072]{1,0:T(8,128)(2,1)S(1)}, u32[]{:S(2)}, u32[]{:S(2)}) collective-permute-start(bf16[192,3072]{1,0:T(8,128)(2,1)S(1)} %constant_dynamic-update-slice_fusion.own), channel_id=1, source_target_pairs={{0,1},{1,0},{2,3},{3,2},{4,5},{5,4},{6,7},{7,6},{8,9},{9,8},{10,11... | collective-permute-start | bytes 3538952 | tf_op jit(solution)/shard_map/ppermute | solution.py:25
  10.8 14.1 %collective-permute-start.1 = (bf16[80,512]{1,0:T(8,128)(2,1)S(1)}, bf16[80,512]{1,0:T(8,128)(2,1)S(1)}, u32[]{:S(2)}, u32[]{:S(2)}) collective-permute-start(bf16[80,512]{1,0:T(8,128)(2,1)S(1)} %copy-done.1), channel_id=1, source_target_pairs={{0,4},{2,6},{4,0},{6,2},{1,5},{3,7},{5,1},{7,3},{8,12},{10,14},{12... | collective-permute-start | bytes 245768 | tf_op jit(solution)/shard_map/ppermute | solution.py:25
  12.8 12.1 %collective-permute-start = (bf16[80,512]{1,0:T(8,128)(2,1)S(1)}, bf16[80,512]{1,0:T(8,128)(2,1)S(1)}, u32[]{:S(2)}, u32[]{:S(2)}) collective-permute-start(bf16[80,512]{1,0:T(8,128)(2,1)S(1)} %copy-done.1), channel_id=1, source_target_pairs={{0,6},{2,0},{4,2},{6,4},{1,7},{3,1},{5,3},{7,5},{8,14},{10,8},{12,... | collective-permute-start | bytes 245768 | tf_op jit(solution)/shard_map/ppermute | solution.py:25
  14.7 10.2 %collective-permute-start.2 = (bf16[80,512]{1,0:T(8,128)(2,1)S(1)}, bf16[80,512]{1,0:T(8,128)(2,1)S(1)}, u32[]{:S(2)}, u32[]{:S(2)}) collective-permute-start(bf16[80,512]{1,0:T(8,128)(2,1)S(1)} %copy-done.1), channel_id=1, source_target_pairs={{0,2},{2,4},{4,6},{6,0},{1,3},{3,5},{5,7},{7,1},{8,10},{10,12},{12... | collective-permute-start | bytes 245768 | tf_op jit(solution)/shard_map/ppermute | solution.py:25
  20.6 22.4 %all-to-all-start = ((bf16[16,160,256]{2,1,0:T(8,128)(2,1)}), bf16[16,160,256]{2,1,0:T(8,128)(2,1)S(1)}, u32[]{:S(2)}, u32[]{:S(2)}) async-start(bf16[16,160,256]{2,1,0:T(8,128)(2,1)} %bitcast.refs_4_), calls=%async_computation | async-start | bytes 2621440 | tf_op jit(solution)/shard_map/all_to_all | solution.py:21
  25.0 39.1 %collective-permute-start.6 = (bf16[4,80,512]{2,1,0:T(8,128)(2,1)S(1)}, bf16[4,80,512]{2,1,0:T(8,128)(2,1)S(1)}, u32[]{:S(2)}, u32[]{:S(2)}) collective-permute-start(bf16[4,80,512]{2,1,0:T(8,128)(2,1)S(1)} %join.1.refs_1_), channel_id=1, source_target_pairs={{0,8},{8,16},{16,24},{24,32},{32,40},{40,48},{48,56},{56,64},{64,7... | collective-permute-start | bytes 983048 | tf_op jit(solution)/shard_map/ppermute | solution.py:25
  27.5 38.7 %collective-permute-start.5 = (bf16[4,80,512]{2,1,0:T(8,128)(2,1)S(1)}, bf16[4,80,512]{2,1,0:T(8,128)(2,1)S(1)}, u32[]{:S(2)}, u32[]{:S(2)}) collective-permute-start(bf16[4,80,512]{2,1,0:T(8,128)(2,1)S(1)} %join.1.refs_1_), channel_id=1, source_target_pairs={{16,0},{113,1},{24,8},{121,9},{32,16},{1,17},{40,24},{9,25},{48,32... | collective-permute-start | bytes 983048 | tf_op jit(solution)/shard_map/ppermute | solution.py:113
  32.4 36.0 %collective-permute-start.4 = (bf16[4,80,512]{2,1,0:T(8,128)(2,1)S(1)}, bf16[4,80,512]{2,1,0:T(8,128)(2,1)S(1)}, u32[]{:S(2)}, u32[]{:S(2)}) collective-permute-start(bf16[4,80,512]{2,1,0:T(8,128)(2,1)S(1)} %join.1.refs_1_), channel_id=1, source_target_pairs={{0,120},{8,0},{16,8},{24,16},{32,24},{40,32},{48,40},{56,48},{64,5... | collective-permute-start | bytes 983048 | tf_op jit(solution)/shard_map/ppermute | solution.py:25
  43.9 33.9 %all-to-all-start.1 = ((bf16[32,8,256]{2,1,0:T(8,128)(2,1)}), bf16[32,8,256]{2,1,0:T(8,128)(2,1)S(1)}, u32[]{:S(2)}, u32[]{:S(2)}) async-start(bf16[32,8,256]{2,1,0:T(8,128)(2,1)} %sum_chips.1), calls=%async_computation.1 | async-start | bytes 262144 | tf_op jit(solution)/shard_map/all_to_all | solution.py:21
  61.9 8.7 %collective-permute-start.7 = (bf16[4,80,512]{2,1,0:T(8,128)(2,1)S(1)}, bf16[4,80,512]{2,1,0:T(8,128)(2,1)S(1)}, u32[]{:S(2)}, u32[]{:S(2)}) collective-permute-start(bf16[4,80,512]{2,1,0:T(8,128)(2,1)S(1)} %join.1.refs_1_), channel_id=1, source_target_pairs={{0,1},{1,0},{2,3},{3,2},{4,5},{5,4},{6,7},{7,6},{8,9},{9,8},{10,11... | collective-permute-start | bytes 983048 | tf_op jit(solution)/shard_map/ppermute | solution.py:25
  64.1 6.6 %collective-permute-start.10 = (bf16[4,80,512]{2,1,0:T(8,128)(2,1)S(1)}, bf16[4,80,512]{2,1,0:T(8,128)(2,1)S(1)}, u32[]{:S(2)}, u32[]{:S(2)}) collective-permute-start(bf16[4,80,512]{2,1,0:T(8,128)(2,1)S(1)} %collective-permute-done.6.refs_4_), channel_id=1, source_target_pairs={{0,1},{1,0},{2,3},{3,2},{4,5},{5,4},{6,7},{7,6},{8,9},{9,8},{10,11... | collective-permute-start | bytes 983048 | tf_op jit(solution)/shard_map/ppermute | solution.py:25
  66.3 4.4 %collective-permute-start.9 = (bf16[4,80,512]{2,1,0:T(8,128)(2,1)S(1)}, bf16[4,80,512]{2,1,0:T(8,128)(2,1)S(1)}, u32[]{:S(2)}, u32[]{:S(2)}) collective-permute-start(bf16[4,80,512]{2,1,0:T(8,128)(2,1)S(1)} %collective-permute-done.5.refs_3_), channel_id=1, source_target_pairs={{0,1},{1,0},{2,3},{3,2},{4,5},{5,4},{6,7},{7,6},{8,9},{9,8},{10,11... | collective-permute-start | bytes 983048 | tf_op jit(solution)/shard_map/ppermute | solution.py:25
  68.4 3.5 %collective-permute-start.8 = (bf16[4,80,512]{2,1,0:T(8,128)(2,1)S(1)}, bf16[4,80,512]{2,1,0:T(8,128)(2,1)S(1)}, u32[]{:S(2)}, u32[]{:S(2)}) collective-permute-start(bf16[4,80,512]{2,1,0:T(8,128)(2,1)S(1)} %collective-permute-done.4.refs_2_), channel_id=1, source_target_pairs={{0,1},{1,0},{2,3},{3,2},{4,5},{5,4},{6,7},{7,6},{8,9},{9,8},{10,11... | collective-permute-start | bytes 983048 | tf_op jit(solution)/shard_map/ppermute | solution.py:25

commit v3 on v2

--- a/solution.py
+++ b/solution.py
@@ -1,3 +1,5 @@
+import functools
+
 import jax
 import jax.numpy as jnp
 from jax import lax
@@ -8,6 +10,8 @@
 X, ZH, ZL, Y, C = 4, 4, 4, 4, 2
 Z = ZH * ZL
 VMEM_LIMIT = 48 * 1024 * 1024
+
+BUSY = pl.CostEstimate(flops=20_000_000_000, bytes_accessed=50_000_000, transcendentals=0)
 
 NT = (((1,), (1,)), ((), ()))
 TN = (((0,), (0,)), ((), ()))
@@ -25,8 +29,7 @@
     return lax.ppermute(a, axes, [(i, (i + step) % size) for i in range(size)])
 
 
-def pair_product(own, other, out, total):
-    depth = own.shape[1] - 512
+def pair_product(depth, own, other, out, total):
     half = pl.ds(pl.multiple_of(depth + lax.axis_index("c") * 256, 128), 256)
     rows = depth // X
     for x in range(X):
@@ -58,18 +61,38 @@
     out[:, 256:] = total[1, :5]
 
 
-def input_product(*refs):
-    grad, out, done = refs[0], refs[-2], refs[-1]
-    me, z, core = lax.axis_index("y"), lax.axis_index("zl"), lax.axis_index("c")
+def hold(weight, after, out):
+    out[...] = weight[...]
+
+
+def own_half(column, out):
+    core = lax.axis_index("c")
     for step in range(ZL):
-        own, other = refs[1 + step], refs[1 + ZL + step]
-        block = []
-        for y in range(Y):
-            at = (y - me + Y) % Y
-            pair = own[at], other[at]
-            block += [jnp.where(core == 0, *pair), jnp.where(core == 0, *pair[::-1])]
-        columns = pl.ds(pl.multiple_of(((z + step) % ZL) * 640, 128), 640)
-        out[:, columns] = dot(grad[...], jnp.concatenate(block, axis=0), NT).astype(jnp.bfloat16)
+        out[step] = jnp.where(core == 0, column[step, 0], column[step, 1])
+
+
+def in_two(near, low, high):
+    low[...] = near[:2]
+    high[...] = near[2:]
+
+
+def input_product(grad, column, near, far, low, high, far_other, out, done):
+    me, core = lax.axis_index("y"), lax.axis_index("c")
+    first = core == 0
+    for step in range(ZL):
+        near_other = (low, high)[step // 2][step % 2]
+        far_two = jnp.where(first, far[step], far_other[step]), jnp.where(first, far_other[step], far[step])
+        ahead = [
+            column[step],
+            jnp.where(first, near[step], near_other),
+            jnp.stack(far_two),
+            jnp.where(first, near_other, near[step]),
+        ]
+        for bit in (1, 2):
+            turned = ahead[-bit:] + ahead[:-bit]
+            ahead = [jnp.where((me & bit) != 0, a, b) for a, b in zip(turned, ahead)]
+        block = jnp.concatenate([rows[c] for rows in ahead for c in range(C)], axis=0)
+        out[:, step * 640 : (step + 1) * 640] = dot(grad[...], block, NT).astype(jnp.bfloat16)
     done[...] = jnp.zeros(done.shape, done.dtype)
 
 
@@ -77,28 +100,21 @@
     return pltpu.CompilerParams(vmem_limit_bytes=limit)
 
 
-def join(pieces, after):
-    def stack(*refs):
-        for i in range(len(pieces)):
-            refs[-1][i] = refs[i][...]
-
-    return pl.pallas_call(
-        stack,
-        in_specs=[pl.BlockSpec(memory_space=pltpu.VMEM)] * len(pieces) + [pl.BlockSpec(memory_space=pl.ANY)],
-        out_shape=jax.ShapeDtypeStruct((len(pieces),) + pieces[0].shape, pieces[0].dtype),
-        compiler_params=params(),
-        cost_estimate=pl.CostEstimate(flops=20_000_000_000, bytes_accessed=50_000_000, transcendentals=0),
-        name="join",
-    )(*pieces, after)
+def call(kernel, outs, *operands, **more):
+    shapes = tuple(jax.ShapeDtypeStruct(out, jnp.bfloat16) for out in outs)
+    name = kernel.__name__
+    return pl.pallas_call(kernel, out_shape=shapes, compiler_params=params(), name=name, **more)(*operands)
 
 
 def body(act, grad, weight):
-    column = [weight, shift(weight, "y", Y - 1, Y), shift(weight, "y", 2, Y), shift(weight, "y", 1, Y)]
+    depth = act.shape[1]
+    width = grad.shape[1]
+    deep = weight.shape[0]
     packed = jnp.concatenate([act, grad], axis=1)
     packed_other = shift(packed, "c", 1, C)
-    rows = act.shape[1] // X
+    rows = depth // X
     partial = pl.pallas_call(
-        pair_product,
+        functools.partial(pair_product, depth),
         out_shape=jax.ShapeDtypeStruct((X * rows, 256), jnp.bfloat16),
         scratch_shapes=[pltpu.VMEM((X, 2, rows, 128), jnp.float32)],
         compiler_params=params(),
@@ -106,12 +122,26 @@
     )(packed, packed_other)
     partial = partial.reshape(X * Y, rows // Y, 256)
     parts = all_to_all(partial, ("x", "y"))
-    column = join(column, partial)
 
-    ring = ("zh", "zl")
-    across = [(((z + 2 - 4 * c) % Z) * C + c, z * C + c) for z in range(Z) for c in range(C)]
-    far = lax.ppermute(column, ring + ("c",), across)
-    own = [column, shift(column, ring, Z - 1, Z), far, shift(column, ring, 1, Z)]
+    def towards(axes, size, step):
+        return axes + ("c",), [(((i + step - 2 * step * c) % size) * C + c, i * C + c) for i in range(size) for c in range(C)]
+
+    def swap(a):
+        return shift(a, "c", 1, C)
+
+    unit = (deep, width)
+    (held,) = call(
+        hold,
+        [unit],
+        weight,
+        partial,
+        in_specs=[pl.BlockSpec(memory_space=pltpu.VMEM), pl.BlockSpec(memory_space=pl.ANY)],
+        cost_estimate=BUSY,
+    )
+    column = lax.all_gather(held, ("zl", "c"), axis=0, tiled=True).reshape((ZL, C) + unit)
+    (half,) = call(own_half, [(ZL,) + unit], column)
+    near = lax.ppermute(column, *towards(("y",), Y, 1))
+    far = lax.ppermute(half, *towards(("y",), Y, 2))
 
     chip_sum = pl.pallas_call(
         sum_chips,
@@ -121,14 +151,14 @@
         name="sum_chips",
     )(parts)
     planes = all_to_all(chip_sum, ("zh", "zl", "c"))
-    other = [shift(piece, "c", 1, C) for piece in own]
 
+    low, high = call(in_two, [(2, C) + unit] * 2, near)
     input_grad, done = pl.pallas_call(
         input_product,
         out_shape=(jax.ShapeDtypeStruct(act.shape, jnp.bfloat16), jax.ShapeDtypeStruct((8, 128), jnp.float32)),
         compiler_params=params(),
         name="input_product",
-    )(grad, *own, *other)
+    )(grad, column, near, far, swap(low), swap(high), swap(far))
     weight_grad = pl.pallas_call(
         sum_planes,
         in_specs=[pl.BlockSpec(memory_space=pltpu.VMEM), pl.BlockSpec(memory_space=pl.ANY)],

time: 78.9 us -> 74.2 us (0.940)
  starting transfers between devices: 61 us -> 40.4 us
  blocking collectives: 0 us -> 15.2 us
    ppermute x10 -> x4, starting transfers between devices: 33.7 us -> 15.3 us  [shift(): return lax.ppermute(a, axes, [(i, (i + step) % size) for i in range(size)])]
    all_gather x0 -> x1, blocking collectives: none -> 15.2 us  [body(): lax.all_gather(held, ('zl', 'c'), axis=0, tiled=True)]
    all_to_all x2, starting transfers between devices: 22.3 us -> 17.3 us  [all_to_all(): return lax.all_to_all(a, axes, split_axis=0, concat_axis=0, tiled=True)]
    ppermute x1 -> x2, starting transfers between devices: 4.9 us -> 7.84 us  [the longest x1 4.36 us: body(): far = lax.ppermute(half, *towards(('y',), Y, 2))]
    ppermute x10 -> x4, waiting for transfers between devices: 1.33 us -> 3.81 us  [shift(): return lax.ppermute(a, axes, [(i, (i + step) % size) for i in range(size)])]
    all_to_all x2, waiting for transfers between devices: 7.84 us -> 5.93 us  [all_to_all(): return lax.all_to_all(a, axes, split_axis=0, concat_axis=0, tiled=True)]
    pallas_call x2 -> x4, Pallas kernels: 2.49 us -> 2.56 us  [the longest x1 2.47 us: body(): pl.pallas_call(functools.partial(pair_product, depth), out_shape=jax.Shap...]
  transfers between devices with their start and end apart: 13 -> 8, of which waited for: 3 -> 3; matrix products, arithmetic and copies ran while one was open for 0% -> 0% of each run, Pallas kernels for 7% -> 4%
where the time goes in v3:
time: 74.2 us; the launch traced here: 73.7 us
  starting transfers between devices  40.4 us (54%)
  blocking collectives  15.2 us (20%)
  waiting for transfers between devices  9.75 us (13%)
  Pallas kernels  6.14 us (8%)
  local copies, waits for them, and re-layouts  1.37 us (2%)
  between operations  0.8 us (1%)
    all_to_all x2, starting transfers between devices, all_to_all(): return lax.all_to_all(a, axes, split_axis=0, concat_axis=0, tiled=True)  17.3 us
    ppermute x4, starting transfers between devices, shift(): return lax.ppermute(a, axes, [(i, (i + step) % size) for i in range(size)])  15.3 us
    all_gather x1, blocking collectives, body(): lax.all_gather(held, ('zl', 'c'), axis=0, tiled=True)  15.2 us
    all_to_all x2, waiting for transfers between devices, all_to_all(): return lax.all_to_all(a, axes, split_axis=0, concat_axis=0, tiled=True)  5.93 us
    ppermute x1, starting transfers between devices, body(): far = lax.ppermute(half, *towards(('y',), Y, 2))  4.36 us
    ppermute x4, waiting for transfers between devices, shift(): return lax.ppermute(a, axes, [(i, (i + step) % size) for i in range(size)])  3.81 us
    ppermute x1, starting transfers between devices, body(): near = lax.ppermute(column, *towards(('y',), Y, 1))  3.48 us
    pallas_call x1, Pallas kernels, body(): pl.pallas_call(functools.partial(pair_product, depth), out_shape=jax.Shap...  2.47 us
  transfers between devices with their start and end apart: 8, of which 3 were waited for; matrix products, arithmetic and copies ran while one was open for 0% of the time, Pallas kernels for 4%

profile of v3, /device:TPU:1, one launch (start us, length us, event | category | flops | bytes accessed | tf_op | source)
XLA Modules:
  0.0 73.7 jit_solution(3061955250737826198)
XLA Ops:
  0.6 0.0 copy-start
  0.6 1.3 %constant_dynamic-update-slice_fusion.1 = bf16[192,3072]{1,0:T(8,128)(2,1)S(1)} fusion(bf16[192,2560]{1,0:T(8,128)(2,1)} %param.3), kind=kLoop, calls=%fused_computation.1 | loop fusion | bytes 1966080
  2.0 0.0 copy-done
  2.0 8.8 %collective-permute-start = (bf16[192,3072]{1,0:T(8,128)(2,1)S(1)}, bf16[192,3072]{1,0:T(8,128)(2,1)S(1)}, u32[]{:S(2)}, u32[]{:S(2)}) collective-permute-start(bf16[192,3072]{1,0:T(8,128)(2,1)S(1)} %constant_dynamic-update-slice_fusion.own), channel_id=1, source_target_pairs={{0,1},{1,0},{2,3},{3,2},{4,5},{5,4},{6,7},{7,6},{8,9},{9,8},{10,11... | collective-permute-start | bytes 3538952 | tf_op jit(solution)/shard_map/ppermute | solution.py:29
  10.8 2.5 %collective-permute-done.other = bf16[192,3072]{1,0:T(8,128)(2,1)S(1)} collective-permute-done((bf16[192,3072]{1,0:T(8,128)(2,1)S(1)}, bf16[192,3072]{1,0:T(8,128)(2,1)S(1)}, u32[]{:S(2)}, u32[]{:S(2)}) %collective-permute-start) | collective-permute-done | bytes 1179680 | tf_op jit(solution)/shard_map/ppermute | solution.py:29
  13.3 2.5 %pair_product.1 = bf16[2560,256]{1,0:T(8,128)(2,1)} custom-call(bf16[192,3072]{1,0:T(8,128)(2,1)S(1)} %constant_dynamic-update-slice_fusion.own, bf16[192,3072]{1,0:T(8,128)(2,1)S(1)} %collective-permute-done.other), custom_call_target="tpu_custom_call" | custom-call | tf_op jit(solution)/shard_map/pair_product/pallas_call | solution.py:116
  15.7 0.0 copy-start.1
  15.7 3.8 %all-to-all-start = ((bf16[16,160,256]{2,1,0:T(8,128)(2,1)}), bf16[16,160,256]{2,1,0:T(8,128)(2,1)S(1)}, u32[]{:S(2)}, u32[]{:S(2)}) async-start(bf16[16,160,256]{2,1,0:T(8,128)(2,1)} %bitcast.after), calls=%async_computation | async-start | bytes 2621440 | tf_op jit(solution)/shard_map/all_to_all | solution.py:25
  19.6 0.0 copy-done.1
  19.6 15.2 %all_gather.3 = bf16[640,512]{1,0:T(8,128)(2,1)S(1)} all-gather(bf16[80,512]{1,0:T(8,128)(2,1)S(1)} %hold.1), channel_id=1, replica_groups=mesh['x'=4,'zh'=4,'zl'=4,'y'=4,'c'=2] {'zl','c'}, dimensions={0}, use_global_device_ids=true | all-gather | bytes 737280 | tf_op jit(solution)/shard_map/all_gather | solution.py:141
  34.8 3.5 %collective-permute-start.1 = (bf16[4,2,80,512]{3,2,1,0:T(8,128)(2,1)S(1)}, bf16[4,2,80,512]{3,2,1,0:T(8,128)(2,1)S(1)}, u32[]{:S(2)}, u32[]{:S(2)}) collective-permute-start(bf16[4,2,80,512]{3,2,1,0:T(8,128)(2,1)S(1)} %bitcast.2), channel_id=1, source_target_pairs={{2,0},{7,1},{4,2},{1,3},{6,4},{3,5},{0,6},{5,7},{10,8},{15,9},{12,... | collective-permute-start | bytes 1966088 | tf_op jit(solution)/shard_map/ppermute | solution.py:143
  38.3 4.4 %collective-permute-start.2 = (bf16[4,80,512]{2,1,0:T(8,128)(2,1)S(1)}, bf16[4,80,512]{2,1,0:T(8,128)(2,1)S(1)}, u32[]{:S(2)}, u32[]{:S(2)}) collective-permute-start(bf16[4,80,512]{2,1,0:T(8,128)(2,1)S(1)} %own_half.1), channel_id=1, source_target_pairs={{4,0},{5,1},{6,2},{7,3},{0,4},{1,5},{2,6},{3,7},{12,8},{13,9},{14,... | collective-permute-start | bytes 983048 | tf_op jit(solution)/shard_map/ppermute | solution.py:144
  42.7 0.0 all-to-all-done.parts
  42.7 1.0 %sum_chips.1 = bf16[32,8,256]{2,1,0:T(8,128)(2,1)} custom-call(bf16[16,160,256]{2,1,0:T(8,128)(2,1)S(1)} %all-to-all-done.parts), custom_call_target="tpu_custom_call" | custom-call | tf_op jit(solution)/shard_map/sum_chips/pallas_call | solution.py:146
  43.7 13.5 %all-to-all-start.1 = ((bf16[32,8,256]{2,1,0:T(8,128)(2,1)}), bf16[32,8,256]{2,1,0:T(8,128)(2,1)S(1)}, u32[]{:S(2)}, u32[]{:S(2)}) async-start(bf16[32,8,256]{2,1,0:T(8,128)(2,1)} %sum_chips.1), calls=%async_computation.1 | async-start | bytes 262144 | tf_op jit(solution)/shard_map/all_to_all | solution.py:25
  57.2 0.0 collective-permute-done.2.far
  57.2 2.1 %collective-permute-start.5 = (bf16[4,80,512]{2,1,0:T(8,128)(2,1)S(1)}, bf16[4,80,512]{2,1,0:T(8,128)(2,1)S(1)}, u32[]{:S(2)}, u32[]{:S(2)}) collective-permute-start(bf16[4,80,512]{2,1,0:T(8,128)(2,1)S(1)} %collective-permute-done.2.far), channel_id=1, source_target_pairs={{0,1},{1,0},{2,3},{3,2},{4,5},{5,4},{6,7},{7,6},{8,9},{9,8},{10,11... | collective-permute-start | bytes 983048 | tf_op jit(solution)/shard_map/ppermute | solution.py:29
  59.3 0.0 collective-permute-done.1.near
  59.4 2.2 %collective-permute-start.3 = (bf16[2,2,80,512]{3,2,1,0:T(8,128)(2,1)S(1)}, bf16[2,2,80,512]{3,2,1,0:T(8,128)(2,1)S(1)}, u32[]{:S(2)}, u32[]{:S(2)}) collective-permute-start(bf16[2,2,80,512]{3,2,1,0:T(8,128)(2,1)S(1)} %get-tuple-element.6), channel_id=1, source_target_pairs={{0,1},{1,0},{2,3},{3,2},{4,5},{5,4},{6,7},{7,6},{8,9},{9,8},{10,11... | collective-permute-start | bytes 983048 | tf_op jit(solution)/shard_map/ppermute | solution.py:29
  61.6 2.1 %collective-permute-start.4 = (bf16[2,2,80,512]{3,2,1,0:T(8,128)(2,1)S(1)}, bf16[2,2,80,512]{3,2,1,0:T(8,128)(2,1)S(1)}, u32[]{:S(2)}, u32[]{:S(2)}) collective-permute-start(bf16[2,2,80,512]{3,2,1,0:T(8,128)(2,1)S(1)} %get-tuple-element.7), channel_id=1, source_target_pairs={{0,1},{1,0},{2,3},{3,2},{4,5},{5,4},{6,7},{7,6},{8,9},{9,8},{10,11... | collective-permute-start | bytes 983048 | tf_op jit(solution)/shard_map/ppermute | solution.py:29
  63.8 0.0 collective-permute-done.5.far_other
  63.8 0.0 collective-permute-done.3.low
  63.8 1.3 %collective-permute-done.4.high = bf16[2,2,80,512]{3,2,1,0:T(8,128)(2,1)S(1)} collective-permute-done((bf16[2,2,80,512]{3,2,1,0:T(8,128)(2,1)S(1)}, bf16[2,2,80,512]{3,2,1,0:T(8,128)(2,1)S(1)}, u32[]{:S(2)}, u32[]{:S(2)}) %collective-permute-start.4) | collective-permute-done | bytes 327712 | tf_op jit(solution)/shard_map/ppermute | solution.py:29
  65.1 2.0 %input_product.1 = (bf16[192,2560]{1,0:T(8,128)(2,1)}, f32[8,128]{1,0:T(8,128)S(1)}) custom-call(bf16[192,512]{1,0:T(8,128)(2,1)S(1)} %copy-done, bf16[4,2,80,512]{3,2,1,0:T(8,128)(2,1)S(1)} %bitcast.4, bf16[4,2,80,512]{3,2,1,0:T(8,128)(2,1)S(1)} %collective-permute-done.1.near, bf16[4,80,512]{2,1,0:T(8,128)(2,1)S(1)} %collective-permute-done.2.far, ...), custom_call_target="tpu_custom_call" | custom-call | tf_op jit(solution)/shard_map/input_product/pallas_call | solution.py:156
  67.1 5.9 %all-to-all-done.1.parts = bf16[32,8,256]{2,1,0:T(8,128)(2,1)S(1)} async-done(((bf16[32,8,256]{2,1,0:T(8,128)(2,1)}), bf16[32,8,256]{2,1,0:T(8,128)(2,1)S(1)}, u32[]{:S(2)}, u32[]{:S(2)}) %all-to-all-start.1) | async-done | bytes 131104 | tf_op jit(solution)/shard_map/all_to_all | solution.py:25
  73.0 0.6 sum_planes.1
  (4 shorter events, 0.1 us)
Async XLA Ops:
  0.6 1.4 %copy-start = (bf16[192,512]{1,0:T(8,128)(2,1)S(1)}, bf16[192,512]{1,0:T(8,128)(2,1)}, u32[]{:S(2)}) copy-start(bf16[192,512]{1,0:T(8,128)(2,1)} %grad.1) | copy-start | bytes 589828
  2.0 11.2 %collective-permute-start = (bf16[192,3072]{1,0:T(8,128)(2,1)S(1)}, bf16[192,3072]{1,0:T(8,128)(2,1)S(1)}, u32[]{:S(2)}, u32[]{:S(2)}) collective-permute-start(bf16[192,3072]{1,0:T(8,128)(2,1)S(1)} %constant_dynamic-update-slice_fusion.own), channel_id=1, source_target_pairs={{0,1},{1,0},{2,3},{3,2},{4,5},{5,4},{6,7},{7,6},{8,9},{9,8},{10,11... | collective-permute-start | bytes 3538952 | tf_op jit(solution)/shard_map/ppermute | solution.py:29
  15.7 3.8 %copy-start.1 = (bf16[80,512]{1,0:T(8,128)(2,1)S(1)}, bf16[80,512]{1,0:T(8,128)(2,1)}, u32[]{:S(2)}) copy-start(bf16[80,512]{1,0:T(8,128)(2,1)} %weight.1) | copy-start | bytes 245764
  15.7 26.9 %all-to-all-start = ((bf16[16,160,256]{2,1,0:T(8,128)(2,1)}), bf16[16,160,256]{2,1,0:T(8,128)(2,1)S(1)}, u32[]{:S(2)}, u32[]{:S(2)}) async-start(bf16[16,160,256]{2,1,0:T(8,128)(2,1)} %bitcast.after), calls=%async_computation | async-start | bytes 2621440 | tf_op jit(solution)/shard_map/all_to_all | solution.py:25
  34.8 24.6 %collective-permute-start.1 = (bf16[4,2,80,512]{3,2,1,0:T(8,128)(2,1)S(1)}, bf16[4,2,80,512]{3,2,1,0:T(8,128)(2,1)S(1)}, u32[]{:S(2)}, u32[]{:S(2)}) collective-permute-start(bf16[4,2,80,512]{3,2,1,0:T(8,128)(2,1)S(1)} %bitcast.2), channel_id=1, source_target_pairs={{2,0},{7,1},{4,2},{1,3},{6,4},{3,5},{0,6},{5,7},{10,8},{15,9},{12,... | collective-permute-start | bytes 1966088 | tf_op jit(solution)/shard_map/ppermute | solution.py:143
  38.3 18.9 %collective-permute-start.2 = (bf16[4,80,512]{2,1,0:T(8,128)(2,1)S(1)}, bf16[4,80,512]{2,1,0:T(8,128)(2,1)S(1)}, u32[]{:S(2)}, u32[]{:S(2)}) collective-permute-start(bf16[4,80,512]{2,1,0:T(8,128)(2,1)S(1)} %own_half.1), channel_id=1, source_target_pairs={{4,0},{5,1},{6,2},{7,3},{0,4},{1,5},{2,6},{3,7},{12,8},{13,9},{14,... | collective-permute-start | bytes 983048 | tf_op jit(solution)/shard_map/ppermute | solution.py:144
  43.7 29.4 %all-to-all-start.1 = ((bf16[32,8,256]{2,1,0:T(8,128)(2,1)}), bf16[32,8,256]{2,1,0:T(8,128)(2,1)S(1)}, u32[]{:S(2)}, u32[]{:S(2)}) async-start(bf16[32,8,256]{2,1,0:T(8,128)(2,1)} %sum_chips.1), calls=%async_computation.1 | async-start | bytes 262144 | tf_op jit(solution)/shard_map/all_to_all | solution.py:25
  57.2 6.6 %collective-permute-start.5 = (bf16[4,80,512]{2,1,0:T(8,128)(2,1)S(1)}, bf16[4,80,512]{2,1,0:T(8,128)(2,1)S(1)}, u32[]{:S(2)}, u32[]{:S(2)}) collective-permute-start(bf16[4,80,512]{2,1,0:T(8,128)(2,1)S(1)} %collective-permute-done.2.far), channel_id=1, source_target_pairs={{0,1},{1,0},{2,3},{3,2},{4,5},{5,4},{6,7},{7,6},{8,9},{9,8},{10,11... | collective-permute-start | bytes 983048 | tf_op jit(solution)/shard_map/ppermute | solution.py:29
  59.4 4.4 %collective-permute-start.3 = (bf16[2,2,80,512]{3,2,1,0:T(8,128)(2,1)S(1)}, bf16[2,2,80,512]{3,2,1,0:T(8,128)(2,1)S(1)}, u32[]{:S(2)}, u32[]{:S(2)}) collective-permute-start(bf16[2,2,80,512]{3,2,1,0:T(8,128)(2,1)S(1)} %get-tuple-element.6), channel_id=1, source_target_pairs={{0,1},{1,0},{2,3},{3,2},{4,5},{5,4},{6,7},{7,6},{8,9},{9,8},{10,11... | collective-permute-start | bytes 983048 | tf_op jit(solution)/shard_map/ppermute | solution.py:29
  61.6 3.5 %collective-permute-start.4 = (bf16[2,2,80,512]{3,2,1,0:T(8,128)(2,1)S(1)}, bf16[2,2,80,512]{3,2,1,0:T(8,128)(2,1)S(1)}, u32[]{:S(2)}, u32[]{:S(2)}) collective-permute-start(bf16[2,2,80,512]{3,2,1,0:T(8,128)(2,1)S(1)} %get-tuple-element.7), channel_id=1, source_target_pairs={{0,1},{1,0},{2,3},{3,2},{4,5},{5,4},{6,7},{7,6},{8,9},{9,8},{10,11... | collective-permute-start | bytes 983048 | tf_op jit(solution)/shard_map/ppermute | solution.py:29

commit v4 on v3

--- a/solution.py
+++ b/solution.py
@@ -13,6 +13,10 @@
 
 BUSY = pl.CostEstimate(flops=20_000_000_000, bytes_accessed=50_000_000, transcendentals=0)
 
+FIRST_Z = 10
+PLANE = list(range(X * Y))[::-1]
+COLUMN = [((FIRST_Z + i) % Z) * C + c for i in range(Z) for c in range(C)]
+
 NT = (((1,), (1,)), ((), ()))
 TN = (((0,), (0,)), ((), ()))
 
@@ -21,8 +25,8 @@
     return lax.dot_general(a, b, dims, preferred_element_type=jnp.float32)
 
 
-def all_to_all(a, axes):
-    return lax.all_to_all(a, axes, split_axis=0, concat_axis=0, tiled=True)
+def all_to_all(a, axes, order):
+    return lax.all_to_all(a, axes, split_axis=0, concat_axis=0, tiled=True, axis_index_groups=[order])
 
 
 def shift(a, axes, step, size):
@@ -39,7 +43,8 @@
             lanes = slice(lane * 128, (lane + 1) * 128)
             total[x, lane] = product[:, lanes]
             for row in range(10 * Y):
-                at = slice(x * rows + row * Z, x * rows + (row + 1) * Z)
+                block, line = PLANE.index(x * Y + row // 10), row % 10
+                at = slice((block * 10 + line) * Z, (block * 10 + line + 1) * Z)
                 out[at, lanes] = total[x, lane, pl.ds(row, Z, stride=10 * Y), :].astype(jnp.bfloat16)
 
 
@@ -52,7 +57,7 @@
         total[lane, rows:] = jnp.zeros((total.shape[1] - rows, 128), jnp.float32)
         for z in range(Z):
             for core in range(C):
-                out[z * C + core, :, lanes] = total[lane, pl.ds(core * 5 * Z + z, 8, stride=Z), :].astype(jnp.bfloat16)
+                out[COLUMN.index(z * C + core), :, lanes] = total[lane, pl.ds(core * 5 * Z + z, 8, stride=Z), :].astype(jnp.bfloat16)
 
 
 def sum_planes(parts, after, out):
@@ -121,7 +126,7 @@
         name="pair_product",
     )(packed, packed_other)
     partial = partial.reshape(X * Y, rows // Y, 256)
-    parts = all_to_all(partial, ("x", "y"))
+    parts = all_to_all(partial, ("x", "y"), PLANE)
 
     def towards(axes, size, step):
         return axes + ("c",), [(((i + step - 2 * step * c) % size) * C + c, i * C + c) for i in range(size) for c in range(C)]
@@ -150,7 +155,7 @@
         compiler_params=params(),
         name="sum_chips",
     )(parts)
-    planes = all_to_all(chip_sum, ("zh", "zl", "c"))
+    planes = all_to_all(chip_sum, ("zh", "zl", "c"), COLUMN)
 
     low, high = call(in_two, [(2, C) + unit] * 2, near)
     input_grad, done = pl.pallas_call(

time: 74.2 us -> 70.3 us (0.947)
  waiting for transfers between devices: 9.75 us -> 3.69 us
  starting transfers between devices: 40.4 us -> 42.1 us
    all_to_all x2, waiting for transfers between devices: 5.93 us -> 0.01 us  [all_to_all(): lax.all_to_all(a, axes, split_axis=0, concat_axis=0, tiled=True, axis_ind...]
    all_to_all x2, starting transfers between devices: 17.3 us -> 21.3 us  [all_to_all(): lax.all_to_all(a, axes, split_axis=0, concat_axis=0, tiled=True, axis_ind...]
    ppermute x1, starting transfers between devices: 4.36 us -> 2.91 us  [body(): far = lax.ppermute(half, *towards(('y',), Y, 2))]
    ppermute x1, starting transfers between devices: 3.48 us -> 2.47 us  [body(): near = lax.ppermute(column, *towards(('y',), Y, 1))]
  transfers between devices with their start and end apart: 8 -> 8, of which waited for: 3 -> 2; matrix products, arithmetic and copies ran while one was open for 0% -> 0% of each run, Pallas kernels for 4% -> 4%
where the time goes in v4:
time: 70.3 us; the launch traced here: 69.8 us
  starting transfers between devices  42.1 us (60%)
  blocking collectives  15.7 us (22%)
  Pallas kernels  6.13 us (9%)
  waiting for transfers between devices  3.69 us (5%)
  local copies, waits for them, and re-layouts  1.37 us (2%)
  between operations  0.79 us (1%)
    all_to_all x2, starting transfers between devices, all_to_all(): lax.all_to_all(a, axes, split_axis=0, concat_axis=0, tiled=True, axis_ind...  21.3 us
    all_gather x1, blocking collectives, body(): lax.all_gather(held, ('zl', 'c'), axis=0, tiled=True)  15.7 us
    ppermute x4, starting transfers between devices, shift(): return lax.ppermute(a, axes, [(i, (i + step) % size) for i in range(size)])  15.4 us
    ppermute x4, waiting for transfers between devices, shift(): return lax.ppermute(a, axes, [(i, (i + step) % size) for i in range(size)])  3.68 us
    ppermute x1, starting transfers between devices, body(): far = lax.ppermute(half, *towards(('y',), Y, 2))  2.91 us
    ppermute x1, starting transfers between devices, body(): near = lax.ppermute(column, *towards(('y',), Y, 1))  2.47 us
    pallas_call x1, Pallas kernels, body(): pl.pallas_call(functools.partial(pair_product, depth), out_shape=jax.Shap...  2.47 us
    pallas_call x1, Pallas kernels, body(): pl.pallas_call(input_product, out_shape=(jax.ShapeDtypeStruct(act.shape,...  1.97 us
  transfers between devices with their start and end apart: 8, of which 2 were waited for; matrix products, arithmetic and copies ran while one was open for 0% of the time, Pallas kernels for 4%

profile of v4, /device:TPU:1, one launch (start us, length us, event | category | flops | bytes accessed | tf_op | source)
XLA Modules:
  0.0 69.8 jit_solution(11846532183454675428)
XLA Ops:
  0.6 0.0 copy-start
  0.6 1.3 %constant_dynamic-update-slice_fusion.1 = bf16[192,3072]{1,0:T(8,128)(2,1)S(1)} fusion(bf16[192,2560]{1,0:T(8,128)(2,1)} %param.3), kind=kLoop, calls=%fused_computation.1 | loop fusion | bytes 1966080
  2.0 0.0 copy-done
  2.0 8.8 %collective-permute-start = (bf16[192,3072]{1,0:T(8,128)(2,1)S(1)}, bf16[192,3072]{1,0:T(8,128)(2,1)S(1)}, u32[]{:S(2)}, u32[]{:S(2)}) collective-permute-start(bf16[192,3072]{1,0:T(8,128)(2,1)S(1)} %constant_dynamic-update-slice_fusion.own), channel_id=1, source_target_pairs={{0,1},{1,0},{2,3},{3,2},{4,5},{5,4},{6,7},{7,6},{8,9},{9,8},{10,11... | collective-permute-start | bytes 3538952 | tf_op jit(solution)/shard_map/ppermute | solution.py:33
  10.8 2.5 %collective-permute-done.other = bf16[192,3072]{1,0:T(8,128)(2,1)S(1)} collective-permute-done((bf16[192,3072]{1,0:T(8,128)(2,1)S(1)}, bf16[192,3072]{1,0:T(8,128)(2,1)S(1)}, u32[]{:S(2)}, u32[]{:S(2)}) %collective-permute-start) | collective-permute-done | bytes 1179680 | tf_op jit(solution)/shard_map/ppermute | solution.py:33
  13.3 2.5 %pair_product.1 = bf16[2560,256]{1,0:T(8,128)(2,1)} custom-call(bf16[192,3072]{1,0:T(8,128)(2,1)S(1)} %constant_dynamic-update-slice_fusion.own, bf16[192,3072]{1,0:T(8,128)(2,1)S(1)} %collective-permute-done.other), custom_call_target="tpu_custom_call" | custom-call | tf_op jit(solution)/shard_map/pair_product/pallas_call | solution.py:121
  15.7 0.0 copy-start.1
  15.7 6.2 %all-to-all-start = ((bf16[16,160,256]{2,1,0:T(8,128)(2,1)}), bf16[16,160,256]{2,1,0:T(8,128)(2,1)S(1)}, u32[]{:S(2)}, u32[]{:S(2)}) async-start(bf16[16,160,256]{2,1,0:T(8,128)(2,1)} %bitcast.after), calls=%async_computation | async-start | bytes 2621440 | tf_op jit(solution)/shard_map/all_to_all | solution.py:29
  22.0 0.0 copy-done.1
  22.0 15.7 %all_gather.3 = bf16[640,512]{1,0:T(8,128)(2,1)S(1)} all-gather(bf16[80,512]{1,0:T(8,128)(2,1)S(1)} %hold.1), channel_id=1, replica_groups=mesh['x'=4,'zh'=4,'zl'=4,'y'=4,'c'=2] {'zl','c'}, dimensions={0}, use_global_device_ids=true | all-gather | bytes 737280 | tf_op jit(solution)/shard_map/all_gather | solution.py:146
  37.7 2.5 %collective-permute-start.1 = (bf16[4,2,80,512]{3,2,1,0:T(8,128)(2,1)S(1)}, bf16[4,2,80,512]{3,2,1,0:T(8,128)(2,1)S(1)}, u32[]{:S(2)}, u32[]{:S(2)}) collective-permute-start(bf16[4,2,80,512]{3,2,1,0:T(8,128)(2,1)S(1)} %bitcast.2), channel_id=1, source_target_pairs={{2,0},{7,1},{4,2},{1,3},{6,4},{3,5},{0,6},{5,7},{10,8},{15,9},{12,... | collective-permute-start | bytes 1966088 | tf_op jit(solution)/shard_map/ppermute | solution.py:148
  40.3 2.9 %collective-permute-start.2 = (bf16[4,80,512]{2,1,0:T(8,128)(2,1)S(1)}, bf16[4,80,512]{2,1,0:T(8,128)(2,1)S(1)}, u32[]{:S(2)}, u32[]{:S(2)}) collective-permute-start(bf16[4,80,512]{2,1,0:T(8,128)(2,1)S(1)} %own_half.1), channel_id=1, source_target_pairs={{4,0},{5,1},{6,2},{7,3},{0,4},{1,5},{2,6},{3,7},{12,8},{13,9},{14,... | collective-permute-start | bytes 983048 | tf_op jit(solution)/shard_map/ppermute | solution.py:149
  43.2 0.0 all-to-all-done.parts
  43.2 1.0 %sum_chips.1 = bf16[32,8,256]{2,1,0:T(8,128)(2,1)} custom-call(bf16[16,160,256]{2,1,0:T(8,128)(2,1)S(1)} %all-to-all-done.parts), custom_call_target="tpu_custom_call" | custom-call | tf_op jit(solution)/shard_map/sum_chips/pallas_call | solution.py:151
  44.2 15.1 %all-to-all-start.1 = ((bf16[32,8,256]{2,1,0:T(8,128)(2,1)}), bf16[32,8,256]{2,1,0:T(8,128)(2,1)S(1)}, u32[]{:S(2)}, u32[]{:S(2)}) async-start(bf16[32,8,256]{2,1,0:T(8,128)(2,1)} %sum_chips.1), calls=%async_computation.1 | async-start | bytes 262144 | tf_op jit(solution)/shard_map/all_to_all | solution.py:29
  59.3 0.0 collective-permute-done.2.far
  59.3 2.3 %collective-permute-start.5 = (bf16[4,80,512]{2,1,0:T(8,128)(2,1)S(1)}, bf16[4,80,512]{2,1,0:T(8,128)(2,1)S(1)}, u32[]{:S(2)}, u32[]{:S(2)}) collective-permute-start(bf16[4,80,512]{2,1,0:T(8,128)(2,1)S(1)} %collective-permute-done.2.far), channel_id=1, source_target_pairs={{0,1},{1,0},{2,3},{3,2},{4,5},{5,4},{6,7},{7,6},{8,9},{9,8},{10,11... | collective-permute-start | bytes 983048 | tf_op jit(solution)/shard_map/ppermute | solution.py:33
  61.6 0.0 collective-permute-done.1.near
  61.6 2.1 %collective-permute-start.3 = (bf16[2,2,80,512]{3,2,1,0:T(8,128)(2,1)S(1)}, bf16[2,2,80,512]{3,2,1,0:T(8,128)(2,1)S(1)}, u32[]{:S(2)}, u32[]{:S(2)}) collective-permute-start(bf16[2,2,80,512]{3,2,1,0:T(8,128)(2,1)S(1)} %get-tuple-element.6), channel_id=1, source_target_pairs={{0,1},{1,0},{2,3},{3,2},{4,5},{5,4},{6,7},{7,6},{8,9},{9,8},{10,11... | collective-permute-start | bytes 983048 | tf_op jit(solution)/shard_map/ppermute | solution.py:33
  63.7 2.3 %collective-permute-start.4 = (bf16[2,2,80,512]{3,2,1,0:T(8,128)(2,1)S(1)}, bf16[2,2,80,512]{3,2,1,0:T(8,128)(2,1)S(1)}, u32[]{:S(2)}, u32[]{:S(2)}) collective-permute-start(bf16[2,2,80,512]{3,2,1,0:T(8,128)(2,1)S(1)} %get-tuple-element.7), channel_id=1, source_target_pairs={{0,1},{1,0},{2,3},{3,2},{4,5},{5,4},{6,7},{7,6},{8,9},{9,8},{10,11... | collective-permute-start | bytes 983048 | tf_op jit(solution)/shard_map/ppermute | solution.py:33
  66.0 0.0 collective-permute-done.5.far_other
  66.0 0.0 collective-permute-done.3.low
  66.0 1.2 %collective-permute-done.4.high = bf16[2,2,80,512]{3,2,1,0:T(8,128)(2,1)S(1)} collective-permute-done((bf16[2,2,80,512]{3,2,1,0:T(8,128)(2,1)S(1)}, bf16[2,2,80,512]{3,2,1,0:T(8,128)(2,1)S(1)}, u32[]{:S(2)}, u32[]{:S(2)}) %collective-permute-start.4) | collective-permute-done | bytes 327712 | tf_op jit(solution)/shard_map/ppermute | solution.py:33
  67.2 2.0 %input_product.1 = (bf16[192,2560]{1,0:T(8,128)(2,1)}, f32[8,128]{1,0:T(8,128)S(1)}) custom-call(bf16[192,512]{1,0:T(8,128)(2,1)S(1)} %copy-done, bf16[4,2,80,512]{3,2,1,0:T(8,128)(2,1)S(1)} %bitcast.4, bf16[4,2,80,512]{3,2,1,0:T(8,128)(2,1)S(1)} %collective-permute-done.1.near, bf16[4,80,512]{2,1,0:T(8,128)(2,1)S(1)} %collective-permute-done.2.far, ...), custom_call_target="tpu_custom_call" | custom-call | tf_op jit(solution)/shard_map/input_product/pallas_call | solution.py:161
  69.2 0.0 all-to-all-done.1.parts
  69.2 0.6 sum_planes.1
  (4 shorter events, 0.1 us)
Async XLA Ops:
  0.6 1.4 %copy-start = (bf16[192,512]{1,0:T(8,128)(2,1)S(1)}, bf16[192,512]{1,0:T(8,128)(2,1)}, u32[]{:S(2)}) copy-start(bf16[192,512]{1,0:T(8,128)(2,1)} %grad.1) | copy-start | bytes 589828
  2.0 11.2 %collective-permute-start = (bf16[192,3072]{1,0:T(8,128)(2,1)S(1)}, bf16[192,3072]{1,0:T(8,128)(2,1)S(1)}, u32[]{:S(2)}, u32[]{:S(2)}) collective-permute-start(bf16[192,3072]{1,0:T(8,128)(2,1)S(1)} %constant_dynamic-update-slice_fusion.own), channel_id=1, source_target_pairs={{0,1},{1,0},{2,3},{3,2},{4,5},{5,4},{6,7},{7,6},{8,9},{9,8},{10,11... | collective-permute-start | bytes 3538952 | tf_op jit(solution)/shard_map/ppermute | solution.py:33
  15.7 6.2 %copy-start.1 = (bf16[80,512]{1,0:T(8,128)(2,1)S(1)}, bf16[80,512]{1,0:T(8,128)(2,1)}, u32[]{:S(2)}) copy-start(bf16[80,512]{1,0:T(8,128)(2,1)} %weight.1) | copy-start | bytes 245764
  15.7 27.4 %all-to-all-start = ((bf16[16,160,256]{2,1,0:T(8,128)(2,1)}), bf16[16,160,256]{2,1,0:T(8,128)(2,1)S(1)}, u32[]{:S(2)}, u32[]{:S(2)}) async-start(bf16[16,160,256]{2,1,0:T(8,128)(2,1)} %bitcast.after), calls=%async_computation | async-start | bytes 2621440 | tf_op jit(solution)/shard_map/all_to_all | solution.py:29
  37.7 23.9 %collective-permute-start.1 = (bf16[4,2,80,512]{3,2,1,0:T(8,128)(2,1)S(1)}, bf16[4,2,80,512]{3,2,1,0:T(8,128)(2,1)S(1)}, u32[]{:S(2)}, u32[]{:S(2)}) collective-permute-start(bf16[4,2,80,512]{3,2,1,0:T(8,128)(2,1)S(1)} %bitcast.2), channel_id=1, source_target_pairs={{2,0},{7,1},{4,2},{1,3},{6,4},{3,5},{0,6},{5,7},{10,8},{15,9},{12,... | collective-permute-start | bytes 1966088 | tf_op jit(solution)/shard_map/ppermute | solution.py:148
  40.3 19.0 %collective-permute-start.2 = (bf16[4,80,512]{2,1,0:T(8,128)(2,1)S(1)}, bf16[4,80,512]{2,1,0:T(8,128)(2,1)S(1)}, u32[]{:S(2)}, u32[]{:S(2)}) collective-permute-start(bf16[4,80,512]{2,1,0:T(8,128)(2,1)S(1)} %own_half.1), channel_id=1, source_target_pairs={{4,0},{5,1},{6,2},{7,3},{0,4},{1,5},{2,6},{3,7},{12,8},{13,9},{14,... | collective-permute-start | bytes 983048 | tf_op jit(solution)/shard_map/ppermute | solution.py:149
  44.2 25.1 %all-to-all-start.1 = ((bf16[32,8,256]{2,1,0:T(8,128)(2,1)}), bf16[32,8,256]{2,1,0:T(8,128)(2,1)S(1)}, u32[]{:S(2)}, u32[]{:S(2)}) async-start(bf16[32,8,256]{2,1,0:T(8,128)(2,1)} %sum_chips.1), calls=%async_computation.1 | async-start | bytes 262144 | tf_op jit(solution)/shard_map/all_to_all | solution.py:29
  59.3 6.7 %collective-permute-start.5 = (bf16[4,80,512]{2,1,0:T(8,128)(2,1)S(1)}, bf16[4,80,512]{2,1,0:T(8,128)(2,1)S(1)}, u32[]{:S(2)}, u32[]{:S(2)}) collective-permute-start(bf16[4,80,512]{2,1,0:T(8,128)(2,1)S(1)} %collective-permute-done.2.far), channel_id=1, source_target_pairs={{0,1},{1,0},{2,3},{3,2},{4,5},{5,4},{6,7},{7,6},{8,9},{9,8},{10,11... | collective-permute-start | bytes 983048 | tf_op jit(solution)/shard_map/ppermute | solution.py:33
  61.6 4.4 %collective-permute-start.3 = (bf16[2,2,80,512]{3,2,1,0:T(8,128)(2,1)S(1)}, bf16[2,2,80,512]{3,2,1,0:T(8,128)(2,1)S(1)}, u32[]{:S(2)}, u32[]{:S(2)}) collective-permute-start(bf16[2,2,80,512]{3,2,1,0:T(8,128)(2,1)S(1)} %get-tuple-element.6), channel_id=1, source_target_pairs={{0,1},{1,0},{2,3},{3,2},{4,5},{5,4},{6,7},{7,6},{8,9},{9,8},{10,11... | collective-permute-start | bytes 983048 | tf_op jit(solution)/shard_map/ppermute | solution.py:33
  63.7 3.5 %collective-permute-start.4 = (bf16[2,2,80,512]{3,2,1,0:T(8,128)(2,1)S(1)}, bf16[2,2,80,512]{3,2,1,0:T(8,128)(2,1)S(1)}, u32[]{:S(2)}, u32[]{:S(2)}) collective-permute-start(bf16[2,2,80,512]{3,2,1,0:T(8,128)(2,1)S(1)} %get-tuple-element.7), channel_id=1, source_target_pairs={{0,1},{1,0},{2,3},{3,2},{4,5},{5,4},{6,7},{7,6},{8,9},{9,8},{10,11... | collective-permute-start | bytes 983048 | tf_op jit(solution)/shard_map/ppermute | solution.py:33

commit v5 on v4

--- a/solution.py
+++ b/solution.py
@@ -33,19 +33,34 @@
     return lax.ppermute(a, axes, [(i, (i + step) % size) for i in range(size)])
 
 
-def pair_product(depth, own, other, out, total):
+def own_product(depth, own, total):
     half = pl.ds(pl.multiple_of(depth + lax.axis_index("c") * 256, 128), 256)
     rows = depth // X
     for x in range(X):
-        columns = slice(x * rows, (x + 1) * rows)
-        product = dot(own[:, columns], own[:, half], TN) + dot(other[:, columns], other[:, half], TN)
+        product = dot(own[:, x * rows : (x + 1) * rows], own[:, half], TN)
+        for lane in range(2):
+            total[x, lane] = product[:, lane * 128 : (lane + 1) * 128]
+
+
+def pair_product(depth, other, before, out, total, ready, sems):
+    half = pl.ds(pl.multiple_of(depth + lax.axis_index("c") * 256, 128), 256)
+    rows = depth // X
+    jobs = []
+    for x in range(X):
+        blocks = [PLANE.index(x * Y + y) for y in range(Y)]
+        product = dot(other[:, x * rows : (x + 1) * rows], other[:, half], TN)
         for lane in range(2):
             lanes = slice(lane * 128, (lane + 1) * 128)
-            total[x, lane] = product[:, lanes]
+            total[x, lane] = product[:, lanes] + before[x, lane]
             for row in range(10 * Y):
-                block, line = PLANE.index(x * Y + row // 10), row % 10
-                at = slice((block * 10 + line) * Z, (block * 10 + line + 1) * Z)
-                out[at, lanes] = total[x, lane, pl.ds(row, Z, stride=10 * Y), :].astype(jnp.bfloat16)
+                place = (blocks[row // 10] - min(blocks)) * 10 + row % 10
+                taken = total[x, lane, pl.ds(row, Z, stride=10 * Y), :]
+                ready[x, place * Z : (place + 1) * Z, lanes] = taken.astype(jnp.bfloat16)
+        target = out.at[pl.ds(min(blocks) * 10 * Z, rows)]
+        jobs.append(pltpu.make_async_copy(ready.at[x], target, sems.at[x]))
+        jobs[-1].start()
+    for job in jobs:
+        job.wait()
 
 
 def sum_chips(parts, out, total):
@@ -118,13 +133,24 @@
     packed = jnp.concatenate([act, grad], axis=1)
     packed_other = shift(packed, "c", 1, C)
     rows = depth // X
+    before = pl.pallas_call(
+        functools.partial(own_product, depth),
+        out_shape=jax.ShapeDtypeStruct((X, 2, rows, 128), jnp.float32),
+        compiler_params=params(),
+        name="own_product",
+    )(packed)
     partial = pl.pallas_call(
         functools.partial(pair_product, depth),
+        out_specs=pl.BlockSpec(memory_space=pl.ANY),
         out_shape=jax.ShapeDtypeStruct((X * rows, 256), jnp.bfloat16),
-        scratch_shapes=[pltpu.VMEM((X, 2, rows, 128), jnp.float32)],
+        scratch_shapes=[
+            pltpu.VMEM((X, 2, rows, 128), jnp.float32),
+            pltpu.VMEM((X, rows, 256), jnp.bfloat16),
+            pltpu.SemaphoreType.DMA((X,)),
+        ],
         compiler_params=params(),
         name="pair_product",
-    )(packed, packed_other)
+    )(packed_other, before)
     partial = partial.reshape(X * Y, rows // Y, 256)
     parts = all_to_all(partial, ("x", "y"), PLANE)
 

time: 70.3 us -> 69.7 us (level)
    pallas_call x1 -> x2, Pallas kernels: 2.47 us -> 2.43 us  [the longest x1 1.87 us: body(): pl.pallas_call(functools.partial(pair_product, depth), out_specs=pl.Block...]
  transfers between devices with their start and end apart: 8 -> 8, of which waited for: 2 -> 2; matrix products, arithmetic and copies ran while one was open for 0% -> 0% of each run, Pallas kernels for 4% -> 5%
where the time goes in v5:
time: 69.7 us; the launch traced here: 69.3 us
  starting transfers between devices  42 us (60%)
  blocking collectives  15.9 us (23%)
  Pallas kernels  6.09 us (9%)
  waiting for transfers between devices  3.13 us (4%)
  local copies, waits for them, and re-layouts  1.38 us (2%)
  between operations  0.81 us (1%)
    all_to_all x2, starting transfers between devices, all_to_all(): lax.all_to_all(a, axes, split_axis=0, concat_axis=0, tiled=True, axis_ind...  21.4 us
    all_gather x1, blocking collectives, body(): lax.all_gather(held, ('zl', 'c'), axis=0, tiled=True)  15.9 us
    ppermute x4, starting transfers between devices, shift(): return lax.ppermute(a, axes, [(i, (i + step) % size) for i in range(size)])  15.4 us
    ppermute x4, waiting for transfers between devices, shift(): return lax.ppermute(a, axes, [(i, (i + step) % size) for i in range(size)])  3.12 us
    ppermute x1, starting transfers between devices, body(): far = lax.ppermute(half, *towards(('y',), Y, 2))  2.78 us
    ppermute x1, starting transfers between devices, body(): near = lax.ppermute(column, *towards(('y',), Y, 1))  2.47 us
    pallas_call x1, Pallas kernels, body(): pl.pallas_call(input_product, out_shape=(jax.ShapeDtypeStruct(act.shape,...  1.97 us
    pallas_call x1, Pallas kernels, body(): pl.pallas_call(functools.partial(pair_product, depth), out_specs=pl.Block...  1.87 us
  transfers between devices with their start and end apart: 8, of which 2 were waited for; matrix products, arithmetic and copies ran while one was open for 0% of the time, Pallas kernels for 5%

profile of v5, /device:TPU:1, one launch (start us, length us, event | category | flops | bytes accessed | tf_op | source)
XLA Modules:
  0.0 69.3 jit_solution(5202282152160081768)
XLA Ops:
  0.6 0.0 copy-start
  0.6 1.3 %constant_dynamic-update-slice_fusion.1 = bf16[192,3072]{1,0:T(8,128)(2,1)S(1)} fusion(bf16[192,2560]{1,0:T(8,128)(2,1)} %param.3), kind=kLoop, calls=%fused_computation.1 | loop fusion | bytes 1966080
  2.0 0.0 copy-done
  2.0 8.8 %collective-permute-start = (bf16[192,3072]{1,0:T(8,128)(2,1)S(1)}, bf16[192,3072]{1,0:T(8,128)(2,1)S(1)}, u32[]{:S(2)}, u32[]{:S(2)}) collective-permute-start(bf16[192,3072]{1,0:T(8,128)(2,1)S(1)} %constant_dynamic-update-slice_fusion.own), channel_id=1, source_target_pairs={{0,1},{1,0},{2,3},{3,2},{4,5},{5,4},{6,7},{7,6},{8,9},{9,8},{10,11... | collective-permute-start | bytes 3538952 | tf_op jit(solution)/shard_map/ppermute | solution.py:33
  10.8 0.6 own_product.1.before
  11.4 1.9 %collective-permute-done.other = bf16[192,3072]{1,0:T(8,128)(2,1)S(1)} collective-permute-done((bf16[192,3072]{1,0:T(8,128)(2,1)S(1)}, bf16[192,3072]{1,0:T(8,128)(2,1)S(1)}, u32[]{:S(2)}, u32[]{:S(2)}) %collective-permute-start) | collective-permute-done | bytes 1179680 | tf_op jit(solution)/shard_map/ppermute | solution.py:33
  13.3 1.9 %pair_product.1 = bf16[2560,256]{1,0:T(8,128)(2,1)} custom-call(bf16[192,3072]{1,0:T(8,128)(2,1)S(1)} %collective-permute-done.other, f32[4,2,640,128]{3,2,1,0:T(8,128)S(1)} %own_product.1.before), custom_call_target="tpu_custom_call" | custom-call | tf_op jit(solution)/shard_map/pair_product/pallas_call | solution.py:142
  15.2 0.0 copy-start.1
  15.2 6.2 %all-to-all-start = ((bf16[16,160,256]{2,1,0:T(8,128)(2,1)}), bf16[16,160,256]{2,1,0:T(8,128)(2,1)S(1)}, u32[]{:S(2)}, u32[]{:S(2)}) async-start(bf16[16,160,256]{2,1,0:T(8,128)(2,1)} %bitcast.after), calls=%async_computation | async-start | bytes 2621440 | tf_op jit(solution)/shard_map/all_to_all | solution.py:29
  21.4 0.0 copy-done.1
  21.4 15.9 %all_gather.3 = bf16[640,512]{1,0:T(8,128)(2,1)S(1)} all-gather(bf16[80,512]{1,0:T(8,128)(2,1)S(1)} %hold.1), channel_id=1, replica_groups=mesh['x'=4,'zh'=4,'zl'=4,'y'=4,'c'=2] {'zl','c'}, dimensions={0}, use_global_device_ids=true | all-gather | bytes 737280 | tf_op jit(solution)/shard_map/all_gather | solution.py:172
  37.3 2.5 %collective-permute-start.1 = (bf16[4,2,80,512]{3,2,1,0:T(8,128)(2,1)S(1)}, bf16[4,2,80,512]{3,2,1,0:T(8,128)(2,1)S(1)}, u32[]{:S(2)}, u32[]{:S(2)}) collective-permute-start(bf16[4,2,80,512]{3,2,1,0:T(8,128)(2,1)S(1)} %bitcast.2), channel_id=1, source_target_pairs={{2,0},{7,1},{4,2},{1,3},{6,4},{3,5},{0,6},{5,7},{10,8},{15,9},{12,... | collective-permute-start | bytes 1966088 | tf_op jit(solution)/shard_map/ppermute | solution.py:174
  39.8 2.8 %collective-permute-start.2 = (bf16[4,80,512]{2,1,0:T(8,128)(2,1)S(1)}, bf16[4,80,512]{2,1,0:T(8,128)(2,1)S(1)}, u32[]{:S(2)}, u32[]{:S(2)}) collective-permute-start(bf16[4,80,512]{2,1,0:T(8,128)(2,1)S(1)} %own_half.1), channel_id=1, source_target_pairs={{4,0},{5,1},{6,2},{7,3},{0,4},{1,5},{2,6},{3,7},{12,8},{13,9},{14,... | collective-permute-start | bytes 983048 | tf_op jit(solution)/shard_map/ppermute | solution.py:175
  42.6 0.0 all-to-all-done.parts
  42.6 1.0 %sum_chips.1 = bf16[32,8,256]{2,1,0:T(8,128)(2,1)} custom-call(bf16[16,160,256]{2,1,0:T(8,128)(2,1)S(1)} %all-to-all-done.parts), custom_call_target="tpu_custom_call" | custom-call | tf_op jit(solution)/shard_map/sum_chips/pallas_call | solution.py:177
  43.6 15.1 %all-to-all-start.1 = ((bf16[32,8,256]{2,1,0:T(8,128)(2,1)}), bf16[32,8,256]{2,1,0:T(8,128)(2,1)S(1)}, u32[]{:S(2)}, u32[]{:S(2)}) async-start(bf16[32,8,256]{2,1,0:T(8,128)(2,1)} %sum_chips.1), calls=%async_computation.1 | async-start | bytes 262144 | tf_op jit(solution)/shard_map/all_to_all | solution.py:29
  58.7 0.0 collective-permute-done.2.far
  58.7 2.3 %collective-permute-start.5 = (bf16[4,80,512]{2,1,0:T(8,128)(2,1)S(1)}, bf16[4,80,512]{2,1,0:T(8,128)(2,1)S(1)}, u32[]{:S(2)}, u32[]{:S(2)}) collective-permute-start(bf16[4,80,512]{2,1,0:T(8,128)(2,1)S(1)} %collective-permute-done.2.far), channel_id=1, source_target_pairs={{0,1},{1,0},{2,3},{3,2},{4,5},{5,4},{6,7},{7,6},{8,9},{9,8},{10,11... | collective-permute-start | bytes 983048 | tf_op jit(solution)/shard_map/ppermute | solution.py:33
  61.0 0.0 collective-permute-done.1.near
  61.1 2.1 %collective-permute-start.3 = (bf16[2,2,80,512]{3,2,1,0:T(8,128)(2,1)S(1)}, bf16[2,2,80,512]{3,2,1,0:T(8,128)(2,1)S(1)}, u32[]{:S(2)}, u32[]{:S(2)}) collective-permute-start(bf16[2,2,80,512]{3,2,1,0:T(8,128)(2,1)S(1)} %get-tuple-element.6), channel_id=1, source_target_pairs={{0,1},{1,0},{2,3},{3,2},{4,5},{5,4},{6,7},{7,6},{8,9},{9,8},{10,11... | collective-permute-start | bytes 983048 | tf_op jit(solution)/shard_map/ppermute | solution.py:33
  63.1 2.3 %collective-permute-start.4 = (bf16[2,2,80,512]{3,2,1,0:T(8,128)(2,1)S(1)}, bf16[2,2,80,512]{3,2,1,0:T(8,128)(2,1)S(1)}, u32[]{:S(2)}, u32[]{:S(2)}) collective-permute-start(bf16[2,2,80,512]{3,2,1,0:T(8,128)(2,1)S(1)} %get-tuple-element.7), channel_id=1, source_target_pairs={{0,1},{1,0},{2,3},{3,2},{4,5},{5,4},{6,7},{7,6},{8,9},{9,8},{10,11... | collective-permute-start | bytes 983048 | tf_op jit(solution)/shard_map/ppermute | solution.py:33
  65.4 0.0 collective-permute-done.5.far_other
  65.4 0.0 collective-permute-done.3.low
  65.4 1.2 %collective-permute-done.4.high = bf16[2,2,80,512]{3,2,1,0:T(8,128)(2,1)S(1)} collective-permute-done((bf16[2,2,80,512]{3,2,1,0:T(8,128)(2,1)S(1)}, bf16[2,2,80,512]{3,2,1,0:T(8,128)(2,1)S(1)}, u32[]{:S(2)}, u32[]{:S(2)}) %collective-permute-start.4) | collective-permute-done | bytes 327712 | tf_op jit(solution)/shard_map/ppermute | solution.py:33
  66.7 2.0 %input_product.1 = (bf16[192,2560]{1,0:T(8,128)(2,1)}, f32[8,128]{1,0:T(8,128)S(1)}) custom-call(bf16[192,512]{1,0:T(8,128)(2,1)S(1)} %copy-done, bf16[4,2,80,512]{3,2,1,0:T(8,128)(2,1)S(1)} %bitcast.4, bf16[4,2,80,512]{3,2,1,0:T(8,128)(2,1)S(1)} %collective-permute-done.1.near, bf16[4,80,512]{2,1,0:T(8,128)(2,1)S(1)} %collective-permute-done.2.far, ...), custom_call_target="tpu_custom_call" | custom-call | tf_op jit(solution)/shard_map/input_product/pallas_call | solution.py:187
  68.6 0.0 all-to-all-done.1.parts
  68.6 0.6 sum_planes.1
  (4 shorter events, 0.1 us)
Async XLA Ops:
  0.6 1.4 %copy-start = (bf16[192,512]{1,0:T(8,128)(2,1)S(1)}, bf16[192,512]{1,0:T(8,128)(2,1)}, u32[]{:S(2)}) copy-start(bf16[192,512]{1,0:T(8,128)(2,1)} %grad.1) | copy-start | bytes 589828
  2.0 11.2 %collective-permute-start = (bf16[192,3072]{1,0:T(8,128)(2,1)S(1)}, bf16[192,3072]{1,0:T(8,128)(2,1)S(1)}, u32[]{:S(2)}, u32[]{:S(2)}) collective-permute-start(bf16[192,3072]{1,0:T(8,128)(2,1)S(1)} %constant_dynamic-update-slice_fusion.own), channel_id=1, source_target_pairs={{0,1},{1,0},{2,3},{3,2},{4,5},{5,4},{6,7},{7,6},{8,9},{9,8},{10,11... | collective-permute-start | bytes 3538952 | tf_op jit(solution)/shard_map/ppermute | solution.py:33
  15.2 6.2 %copy-start.1 = (bf16[80,512]{1,0:T(8,128)(2,1)S(1)}, bf16[80,512]{1,0:T(8,128)(2,1)}, u32[]{:S(2)}) copy-start(bf16[80,512]{1,0:T(8,128)(2,1)} %weight.1) | copy-start | bytes 245764
  15.2 27.4 %all-to-all-start = ((bf16[16,160,256]{2,1,0:T(8,128)(2,1)}), bf16[16,160,256]{2,1,0:T(8,128)(2,1)S(1)}, u32[]{:S(2)}, u32[]{:S(2)}) async-start(bf16[16,160,256]{2,1,0:T(8,128)(2,1)} %bitcast.after), calls=%async_computation | async-start | bytes 2621440 | tf_op jit(solution)/shard_map/all_to_all | solution.py:29
  37.3 23.7 %collective-permute-start.1 = (bf16[4,2,80,512]{3,2,1,0:T(8,128)(2,1)S(1)}, bf16[4,2,80,512]{3,2,1,0:T(8,128)(2,1)S(1)}, u32[]{:S(2)}, u32[]{:S(2)}) collective-permute-start(bf16[4,2,80,512]{3,2,1,0:T(8,128)(2,1)S(1)} %bitcast.2), channel_id=1, source_target_pairs={{2,0},{7,1},{4,2},{1,3},{6,4},{3,5},{0,6},{5,7},{10,8},{15,9},{12,... | collective-permute-start | bytes 1966088 | tf_op jit(solution)/shard_map/ppermute | solution.py:174
  39.8 18.9 %collective-permute-start.2 = (bf16[4,80,512]{2,1,0:T(8,128)(2,1)S(1)}, bf16[4,80,512]{2,1,0:T(8,128)(2,1)S(1)}, u32[]{:S(2)}, u32[]{:S(2)}) collective-permute-start(bf16[4,80,512]{2,1,0:T(8,128)(2,1)S(1)} %own_half.1), channel_id=1, source_target_pairs={{4,0},{5,1},{6,2},{7,3},{0,4},{1,5},{2,6},{3,7},{12,8},{13,9},{14,... | collective-permute-start | bytes 983048 | tf_op jit(solution)/shard_map/ppermute | solution.py:175
  43.6 25.1 %all-to-all-start.1 = ((bf16[32,8,256]{2,1,0:T(8,128)(2,1)}), bf16[32,8,256]{2,1,0:T(8,128)(2,1)S(1)}, u32[]{:S(2)}, u32[]{:S(2)}) async-start(bf16[32,8,256]{2,1,0:T(8,128)(2,1)} %sum_chips.1), calls=%async_computation.1 | async-start | bytes 262144 | tf_op jit(solution)/shard_map/all_to_all | solution.py:29
  58.7 6.7 %collective-permute-start.5 = (bf16[4,80,512]{2,1,0:T(8,128)(2,1)S(1)}, bf16[4,80,512]{2,1,0:T(8,128)(2,1)S(1)}, u32[]{:S(2)}, u32[]{:S(2)}) collective-permute-start(bf16[4,80,512]{2,1,0:T(8,128)(2,1)S(1)} %collective-permute-done.2.far), channel_id=1, source_target_pairs={{0,1},{1,0},{2,3},{3,2},{4,5},{5,4},{6,7},{7,6},{8,9},{9,8},{10,11... | collective-permute-start | bytes 983048 | tf_op jit(solution)/shard_map/ppermute | solution.py:33
  61.1 4.4 %collective-permute-start.3 = (bf16[2,2,80,512]{3,2,1,0:T(8,128)(2,1)S(1)}, bf16[2,2,80,512]{3,2,1,0:T(8,128)(2,1)S(1)}, u32[]{:S(2)}, u32[]{:S(2)}) collective-permute-start(bf16[2,2,80,512]{3,2,1,0:T(8,128)(2,1)S(1)} %get-tuple-element.6), channel_id=1, source_target_pairs={{0,1},{1,0},{2,3},{3,2},{4,5},{5,4},{6,7},{7,6},{8,9},{9,8},{10,11... | collective-permute-start | bytes 983048 | tf_op jit(solution)/shard_map/ppermute | solution.py:33
  63.1 3.5 %collective-permute-start.4 = (bf16[2,2,80,512]{3,2,1,0:T(8,128)(2,1)S(1)}, bf16[2,2,80,512]{3,2,1,0:T(8,128)(2,1)S(1)}, u32[]{:S(2)}, u32[]{:S(2)}) collective-permute-start(bf16[2,2,80,512]{3,2,1,0:T(8,128)(2,1)S(1)} %get-tuple-element.7), channel_id=1, source_target_pairs={{0,1},{1,0},{2,3},{3,2},{4,5},{5,4},{6,7},{7,6},{8,9},{9,8},{10,11... | collective-permute-start | bytes 983048 | tf_op jit(solution)/shard_map/ppermute | solution.py:33

commit v6 on v5

--- a/solution.py
+++ b/solution.py
@@ -10,6 +10,7 @@
 X, ZH, ZL, Y, C = 4, 4, 4, 4, 2
 Z = ZH * ZL
 VMEM_LIMIT = 48 * 1024 * 1024
+PACK_LIMIT = 62_200_000
 
 BUSY = pl.CostEstimate(flops=20_000_000_000, bytes_accessed=50_000_000, transcendentals=0)
 
@@ -120,6 +121,30 @@
     return pltpu.CompilerParams(vmem_limit_bytes=limit)
 
 
+def pack(act, grad):
+    depth, width = act.shape[1], grad.shape[1]
+
+    def kernel(act, grad, out, sems):
+        jobs = [
+            pltpu.make_async_copy(act, out.at[:, :depth], sems.at[0]),
+            pltpu.make_async_copy(grad, out.at[:, depth:], sems.at[1]),
+        ]
+        for job in jobs:
+            job.start()
+        for job in jobs:
+            job.wait()
+
+    return pl.pallas_call(
+        kernel,
+        in_specs=[pl.BlockSpec(memory_space=pl.ANY)] * 2,
+        out_specs=pl.BlockSpec(memory_space=pl.ANY),
+        out_shape=jax.ShapeDtypeStruct((act.shape[0], depth + width), act.dtype),
+        scratch_shapes=[pltpu.SemaphoreType.DMA((2,))],
+        compiler_params=params(PACK_LIMIT),
+        name="pack",
+    )(act, grad)
+
+
 def call(kernel, outs, *operands, **more):
     shapes = tuple(jax.ShapeDtypeStruct(out, jnp.bfloat16) for out in outs)
     name = kernel.__name__
@@ -130,7 +155,7 @@
     depth = act.shape[1]
     width = grad.shape[1]
     deep = weight.shape[0]
-    packed = jnp.concatenate([act, grad], axis=1)
+    packed = pack(act, grad)
     packed_other = shift(packed, "c", 1, C)
     rows = depth // X
     before = pl.pallas_call(

time: 69.7 us -> 106 us (1.52)
  Pallas kernels: 6.09 us -> 43 us
  waiting for transfers between devices: 3.13 us -> 2.07 us
    pallas_call x0 -> x1, Pallas kernels: none -> 36.9 us  [pack(): pl.pallas_call(kernel, in_specs=[pl.BlockSpec(memory_space=pl.ANY)] * 2,...]
    ppermute x4, waiting for transfers between devices: 3.12 us -> 2.05 us  [shift(): return lax.ppermute(a, axes, [(i, (i + step) % size) for i in range(size)])]
  transfers between devices with their start and end apart: 8 -> 8, of which waited for: 2 -> 2; matrix products, arithmetic and copies ran while one was open for 0% -> 0% of each run, Pallas kernels for 5% -> 3%
where the time goes in v6:
time: 106 us; the launch traced here: 105 us
  Pallas kernels  43 us (41%)
  starting transfers between devices  42.1 us (40%)
  blocking collectives  15.9 us (15%)
  waiting for transfers between devices  2.07 us (2%)
  local copies, waits for them, and re-layouts  1.28 us (1%)
    pallas_call x1, Pallas kernels, pack(): pl.pallas_call(kernel, in_specs=[pl.BlockSpec(memory_space=pl.ANY)] * 2,...  36.9 us
    all_to_all x2, starting transfers between devices, all_to_all(): lax.all_to_all(a, axes, split_axis=0, concat_axis=0, tiled=True, axis_ind...  21.4 us
    all_gather x1, blocking collectives, body(): lax.all_gather(held, ('zl', 'c'), axis=0, tiled=True)  15.9 us
    ppermute x4, starting transfers between devices, shift(): return lax.ppermute(a, axes, [(i, (i + step) % size) for i in range(size)])  15.4 us
    ppermute x1, starting transfers between devices, body(): far = lax.ppermute(half, *towards(('y',), Y, 2))  2.92 us
    ppermute x1, starting transfers between devices, body(): near = lax.ppermute(column, *towards(('y',), Y, 1))  2.47 us
  transfers between devices with their start and end apart: 8, of which 2 were waited for; matrix products, arithmetic and copies ran while one was open for 0% of the time, Pallas kernels for 3%

profile of v6, /device:TPU:1, one launch (start us, length us, event | category | flops | bytes accessed | tf_op | source)
XLA Modules:
  0.0 105.1 jit_solution(13381906368795549756)
XLA Ops:
  0.6 36.9 %pack.1.own = bf16[192,3072]{1,0:T(8,128)(2,1)} custom-call(bf16[192,2560]{1,0:T(8,128)(2,1)} %act.1, bf16[192,512]{1,0:T(8,128)(2,1)} %grad.3), custom_call_target="tpu_custom_call" | custom-call | tf_op jit(solution)/shard_map/pack/pallas_call | solution.py:137
  37.5 8.8 %collective-permute-start = (bf16[192,3072]{1,0:T(8,128)(2,1)}, bf16[192,3072]{1,0:T(8,128)(2,1)S(1)}, u32[]{:S(2)}, u32[]{:S(2)}) collective-permute-start(bf16[192,3072]{1,0:T(8,128)(2,1)} %pack.1.own), channel_id=1, source_target_pairs={{0,1},{1,0},{2,3},{3,2},{4,5},{5,4},{6,7},{7,6},{8,9},{9,8},{10,11... | collective-permute-start | bytes 3538952 | tf_op jit(solution)/shard_map/ppermute | solution.py:34
  46.3 0.0 copy-start
  46.3 1.3 %copy-done = bf16[192,3072]{1,0:T(8,128)(2,1)S(1)} copy-done((bf16[192,3072]{1,0:T(8,128)(2,1)S(1)}, bf16[192,3072]{1,0:T(8,128)(2,1)}, u32[]{:S(2)}) %copy-start) | copy-done | bytes 1179672
  47.6 0.6 own_product.1.before
  48.1 0.8 collective-permute-done.other
  48.9 1.9 %pair_product.1 = bf16[2560,256]{1,0:T(8,128)(2,1)} custom-call(bf16[192,3072]{1,0:T(8,128)(2,1)S(1)} %collective-permute-done.other, f32[4,2,640,128]{3,2,1,0:T(8,128)S(1)} %own_product.1.before), custom_call_target="tpu_custom_call" | custom-call | tf_op jit(solution)/shard_map/pair_product/pallas_call | solution.py:167
  50.8 0.0 copy-start.2
  50.8 6.2 %all-to-all-start = ((bf16[16,160,256]{2,1,0:T(8,128)(2,1)}), bf16[16,160,256]{2,1,0:T(8,128)(2,1)S(1)}, u32[]{:S(2)}, u32[]{:S(2)}) async-start(bf16[16,160,256]{2,1,0:T(8,128)(2,1)} %bitcast.after), calls=%async_computation | async-start | bytes 2621440 | tf_op jit(solution)/shard_map/all_to_all | solution.py:30
  57.1 0.0 copy-done.2
  57.1 15.9 %all_gather.3 = bf16[640,512]{1,0:T(8,128)(2,1)S(1)} all-gather(bf16[80,512]{1,0:T(8,128)(2,1)S(1)} %hold.1), channel_id=1, replica_groups=mesh['x'=4,'zh'=4,'zl'=4,'y'=4,'c'=2] {'zl','c'}, dimensions={0}, use_global_device_ids=true | all-gather | bytes 737280 | tf_op jit(solution)/shard_map/all_gather | solution.py:197
  73.0 2.5 %collective-permute-start.1 = (bf16[4,2,80,512]{3,2,1,0:T(8,128)(2,1)S(1)}, bf16[4,2,80,512]{3,2,1,0:T(8,128)(2,1)S(1)}, u32[]{:S(2)}, u32[]{:S(2)}) collective-permute-start(bf16[4,2,80,512]{3,2,1,0:T(8,128)(2,1)S(1)} %bitcast.2), channel_id=1, source_target_pairs={{2,0},{7,1},{4,2},{1,3},{6,4},{3,5},{0,6},{5,7},{10,8},{15,9},{12,... | collective-permute-start | bytes 1966088 | tf_op jit(solution)/shard_map/ppermute | solution.py:199
  75.5 0.0 copy-start.1
  75.5 2.9 %collective-permute-start.2 = (bf16[4,80,512]{2,1,0:T(8,128)(2,1)S(1)}, bf16[4,80,512]{2,1,0:T(8,128)(2,1)S(1)}, u32[]{:S(2)}, u32[]{:S(2)}) collective-permute-start(bf16[4,80,512]{2,1,0:T(8,128)(2,1)S(1)} %own_half.1), channel_id=1, source_target_pairs={{4,0},{5,1},{6,2},{7,3},{0,4},{1,5},{2,6},{3,7},{12,8},{13,9},{14,... | collective-permute-start | bytes 983048 | tf_op jit(solution)/shard_map/ppermute | solution.py:200
  78.4 0.0 all-to-all-done.parts
  78.4 1.0 sum_chips.1
  79.4 15.1 %all-to-all-start.1 = ((bf16[32,8,256]{2,1,0:T(8,128)(2,1)}), bf16[32,8,256]{2,1,0:T(8,128)(2,1)S(1)}, u32[]{:S(2)}, u32[]{:S(2)}) async-start(bf16[32,8,256]{2,1,0:T(8,128)(2,1)} %sum_chips.1), calls=%async_computation.1 | async-start | bytes 262144 | tf_op jit(solution)/shard_map/all_to_all | solution.py:30
  94.6 0.0 collective-permute-done.2.far
  94.6 2.3 %collective-permute-start.5 = (bf16[4,80,512]{2,1,0:T(8,128)(2,1)S(1)}, bf16[4,80,512]{2,1,0:T(8,128)(2,1)S(1)}, u32[]{:S(2)}, u32[]{:S(2)}) collective-permute-start(bf16[4,80,512]{2,1,0:T(8,128)(2,1)S(1)} %collective-permute-done.2.far), channel_id=1, source_target_pairs={{0,1},{1,0},{2,3},{3,2},{4,5},{5,4},{6,7},{7,6},{8,9},{9,8},{10,11... | collective-permute-start | bytes 983048 | tf_op jit(solution)/shard_map/ppermute | solution.py:34
  96.8 0.0 collective-permute-done.1.near
  96.9 2.1 %collective-permute-start.3 = (bf16[2,2,80,512]{3,2,1,0:T(8,128)(2,1)S(1)}, bf16[2,2,80,512]{3,2,1,0:T(8,128)(2,1)S(1)}, u32[]{:S(2)}, u32[]{:S(2)}) collective-permute-start(bf16[2,2,80,512]{3,2,1,0:T(8,128)(2,1)S(1)} %get-tuple-element.6), channel_id=1, source_target_pairs={{0,1},{1,0},{2,3},{3,2},{4,5},{5,4},{6,7},{7,6},{8,9},{9,8},{10,11... | collective-permute-start | bytes 983048 | tf_op jit(solution)/shard_map/ppermute | solution.py:34
  99.0 2.3 %collective-permute-start.4 = (bf16[2,2,80,512]{3,2,1,0:T(8,128)(2,1)S(1)}, bf16[2,2,80,512]{3,2,1,0:T(8,128)(2,1)S(1)}, u32[]{:S(2)}, u32[]{:S(2)}) collective-permute-start(bf16[2,2,80,512]{3,2,1,0:T(8,128)(2,1)S(1)} %get-tuple-element.7), channel_id=1, source_target_pairs={{0,1},{1,0},{2,3},{3,2},{4,5},{5,4},{6,7},{7,6},{8,9},{9,8},{10,11... | collective-permute-start | bytes 983048 | tf_op jit(solution)/shard_map/ppermute | solution.py:34
  101.2 0.0 collective-permute-done.5.far_other
  101.3 0.0 collective-permute-done.3.low
  101.3 1.2 %collective-permute-done.4.high = bf16[2,2,80,512]{3,2,1,0:T(8,128)(2,1)S(1)} collective-permute-done((bf16[2,2,80,512]{3,2,1,0:T(8,128)(2,1)S(1)}, bf16[2,2,80,512]{3,2,1,0:T(8,128)(2,1)S(1)}, u32[]{:S(2)}, u32[]{:S(2)}) %collective-permute-start.4) | collective-permute-done | bytes 327712 | tf_op jit(solution)/shard_map/ppermute | solution.py:34
  102.5 0.0 copy-done.1
  102.5 2.0 %input_product.1 = (bf16[192,2560]{1,0:T(8,128)(2,1)}, f32[8,128]{1,0:T(8,128)S(1)}) custom-call(bf16[192,512]{1,0:T(8,128)(2,1)S(1)} %copy-done.1, bf16[4,2,80,512]{3,2,1,0:T(8,128)(2,1)S(1)} %bitcast.4, bf16[4,2,80,512]{3,2,1,0:T(8,128)(2,1)S(1)} %collective-permute-done.1.near, bf16[4,80,512]{2,1,0:T(8,128)(2,1)S(1)} %collective-permute-done.2.far, ...), custom_call_target="tpu_custom_call" | custom-call | tf_op jit(solution)/shard_map/input_product/pallas_call | solution.py:212
  104.5 0.0 all-to-all-done.1.parts
  104.5 0.6 sum_planes.1
  (3 shorter events, 0.1 us)
Async XLA Ops:
  37.5 11.5 %collective-permute-start = (bf16[192,3072]{1,0:T(8,128)(2,1)}, bf16[192,3072]{1,0:T(8,128)(2,1)S(1)}, u32[]{:S(2)}, u32[]{:S(2)}) collective-permute-start(bf16[192,3072]{1,0:T(8,128)(2,1)} %pack.1.own), channel_id=1, source_target_pairs={{0,1},{1,0},{2,3},{3,2},{4,5},{5,4},{6,7},{7,6},{8,9},{9,8},{10,11... | collective-permute-start | bytes 3538952 | tf_op jit(solution)/shard_map/ppermute | solution.py:34
  46.3 1.3 %copy-start = (bf16[192,3072]{1,0:T(8,128)(2,1)S(1)}, bf16[192,3072]{1,0:T(8,128)(2,1)}, u32[]{:S(2)}) copy-start(bf16[192,3072]{1,0:T(8,128)(2,1)} %pack.1.own) | copy-start | bytes 3538948
  50.8 6.2 %copy-start.2 = (bf16[80,512]{1,0:T(8,128)(2,1)S(1)}, bf16[80,512]{1,0:T(8,128)(2,1)}, u32[]{:S(2)}) copy-start(bf16[80,512]{1,0:T(8,128)(2,1)} %weight.1) | copy-start | bytes 245764
  50.8 27.6 %all-to-all-start = ((bf16[16,160,256]{2,1,0:T(8,128)(2,1)}), bf16[16,160,256]{2,1,0:T(8,128)(2,1)S(1)}, u32[]{:S(2)}, u32[]{:S(2)}) async-start(bf16[16,160,256]{2,1,0:T(8,128)(2,1)} %bitcast.after), calls=%async_computation | async-start | bytes 2621440 | tf_op jit(solution)/shard_map/all_to_all | solution.py:30
  73.0 23.9 %collective-permute-start.1 = (bf16[4,2,80,512]{3,2,1,0:T(8,128)(2,1)S(1)}, bf16[4,2,80,512]{3,2,1,0:T(8,128)(2,1)S(1)}, u32[]{:S(2)}, u32[]{:S(2)}) collective-permute-start(bf16[4,2,80,512]{3,2,1,0:T(8,128)(2,1)S(1)} %bitcast.2), channel_id=1, source_target_pairs={{2,0},{7,1},{4,2},{1,3},{6,4},{3,5},{0,6},{5,7},{10,8},{15,9},{12,... | collective-permute-start | bytes 1966088 | tf_op jit(solution)/shard_map/ppermute | solution.py:199
  75.5 27.0 %copy-start.1 = (bf16[192,512]{1,0:T(8,128)(2,1)S(1)}, bf16[192,512]{1,0:T(8,128)(2,1)}, u32[]{:S(2)}) copy-start(bf16[192,512]{1,0:T(8,128)(2,1)} %grad.3) | copy-start | bytes 589828
  75.5 19.1 %collective-permute-start.2 = (bf16[4,80,512]{2,1,0:T(8,128)(2,1)S(1)}, bf16[4,80,512]{2,1,0:T(8,128)(2,1)S(1)}, u32[]{:S(2)}, u32[]{:S(2)}) collective-permute-start(bf16[4,80,512]{2,1,0:T(8,128)(2,1)S(1)} %own_half.1), channel_id=1, source_target_pairs={{4,0},{5,1},{6,2},{7,3},{0,4},{1,5},{2,6},{3,7},{12,8},{13,9},{14,... | collective-permute-start | bytes 983048 | tf_op jit(solution)/shard_map/ppermute | solution.py:200
  79.4 25.1 %all-to-all-start.1 = ((bf16[32,8,256]{2,1,0:T(8,128)(2,1)}), bf16[32,8,256]{2,1,0:T(8,128)(2,1)S(1)}, u32[]{:S(2)}, u32[]{:S(2)}) async-start(bf16[32,8,256]{2,1,0:T(8,128)(2,1)} %sum_chips.1), calls=%async_computation.1 | async-start | bytes 262144 | tf_op jit(solution)/shard_map/all_to_all | solution.py:30
  94.6 6.7 %collective-permute-start.5 = (bf16[4,80,512]{2,1,0:T(8,128)(2,1)S(1)}, bf16[4,80,512]{2,1,0:T(8,128)(2,1)S(1)}, u32[]{:S(2)}, u32[]{:S(2)}) collective-permute-start(bf16[4,80,512]{2,1,0:T(8,128)(2,1)S(1)} %collective-permute-done.2.far), channel_id=1, source_target_pairs={{0,1},{1,0},{2,3},{3,2},{4,5},{5,4},{6,7},{7,6},{8,9},{9,8},{10,11... | collective-permute-start | bytes 983048 | tf_op jit(solution)/shard_map/ppermute | solution.py:34
  96.9 4.4 %collective-permute-start.3 = (bf16[2,2,80,512]{3,2,1,0:T(8,128)(2,1)S(1)}, bf16[2,2,80,512]{3,2,1,0:T(8,128)(2,1)S(1)}, u32[]{:S(2)}, u32[]{:S(2)}) collective-permute-start(bf16[2,2,80,512]{3,2,1,0:T(8,128)(2,1)S(1)} %get-tuple-element.6), channel_id=1, source_target_pairs={{0,1},{1,0},{2,3},{3,2},{4,5},{5,4},{6,7},{7,6},{8,9},{9,8},{10,11... | collective-permute-start | bytes 983048 | tf_op jit(solution)/shard_map/ppermute | solution.py:34
  99.0 3.5 %collective-permute-start.4 = (bf16[2,2,80,512]{3,2,1,0:T(8,128)(2,1)S(1)}, bf16[2,2,80,512]{3,2,1,0:T(8,128)(2,1)S(1)}, u32[]{:S(2)}, u32[]{:S(2)}) collective-permute-start(bf16[2,2,80,512]{3,2,1,0:T(8,128)(2,1)S(1)} %get-tuple-element.7), channel_id=1, source_target_pairs={{0,1},{1,0},{2,3},{3,2},{4,5},{5,4},{6,7},{7,6},{8,9},{9,8},{10,11... | collective-permute-start | bytes 983048 | tf_op jit(solution)/shard_map/ppermute | solution.py:34

commit v7 on v6

--- a/solution.py
+++ b/solution.py
@@ -137,7 +137,7 @@
     return pl.pallas_call(
         kernel,
         in_specs=[pl.BlockSpec(memory_space=pl.ANY)] * 2,
-        out_specs=pl.BlockSpec(memory_space=pl.ANY),
+        out_specs=pl.BlockSpec(memory_space=pltpu.VMEM),
         out_shape=jax.ShapeDtypeStruct((act.shape[0], depth + width), act.dtype),
         scratch_shapes=[pltpu.SemaphoreType.DMA((2,))],
         compiler_params=params(PACK_LIMIT),

time: 106 us -> 71 us (0.67)
  Pallas kernels: 43 us -> 8.38 us
    pallas_call x1, Pallas kernels: 36.9 us -> 2.28 us  [pack(): pl.pallas_call(kernel, in_specs=[pl.BlockSpec(memory_space=pl.ANY)] * 2,...]
  transfers between devices with their start and end apart: 8 -> 8, of which waited for: 2 -> 2; matrix products, arithmetic and copies ran while one was open for 0% -> 0% of each run, Pallas kernels for 3% -> 5%
where the time goes in v7:
time: 71 us; the launch traced here: 70.5 us
  starting transfers between devices  42.3 us (60%)
  blocking collectives  15.7 us (22%)
  Pallas kernels  8.38 us (12%)
  waiting for transfers between devices  2.06 us (3%)
  local copies, waits for them, and re-layouts  1.28 us (2%)
  between operations  0.8 us (1%)
    all_to_all x2, starting transfers between devices, all_to_all(): lax.all_to_all(a, axes, split_axis=0, concat_axis=0, tiled=True, axis_ind...  21.4 us
    all_gather x1, blocking collectives, body(): lax.all_gather(held, ('zl', 'c'), axis=0, tiled=True)  15.7 us
    ppermute x4, starting transfers between devices, shift(): return lax.ppermute(a, axes, [(i, (i + step) % size) for i in range(size)])  15.4 us
    ppermute x1, starting transfers between devices, body(): far = lax.ppermute(half, *towards(('y',), Y, 2))  3.04 us
    ppermute x1, starting transfers between devices, body(): near = lax.ppermute(column, *towards(('y',), Y, 1))  2.48 us
    pallas_call x1, Pallas kernels, pack(): pl.pallas_call(kernel, in_specs=[pl.BlockSpec(memory_space=pl.ANY)] * 2,...  2.28 us
    ppermute x4, waiting for transfers between devices, shift(): return lax.ppermute(a, axes, [(i, (i + step) % size) for i in range(size)])  2.05 us
    pallas_call x1, Pallas kernels, body(): pl.pallas_call(input_product, out_shape=(jax.ShapeDtypeStruct(act.shape,...  1.97 us
  transfers between devices with their start and end apart: 8, of which 2 were waited for; matrix products, arithmetic and copies ran while one was open for 0% of the time, Pallas kernels for 5%

profile of v7, /device:TPU:1, one launch (start us, length us, event | category | flops | bytes accessed | tf_op | source)
XLA Modules:
  0.0 70.5 jit_solution(884298618350070895)
XLA Ops:
  0.6 2.3 %pack.1.own = bf16[192,3072]{1,0:T(8,128)(2,1)} custom-call(bf16[192,2560]{1,0:T(8,128)(2,1)} %act.1, bf16[192,512]{1,0:T(8,128)(2,1)} %grad.3), custom_call_target="tpu_custom_call" | custom-call | tf_op jit(solution)/shard_map/pack/pallas_call | solution.py:137
  2.9 8.8 %collective-permute-start = (bf16[192,3072]{1,0:T(8,128)(2,1)}, bf16[192,3072]{1,0:T(8,128)(2,1)S(1)}, u32[]{:S(2)}, u32[]{:S(2)}) collective-permute-start(bf16[192,3072]{1,0:T(8,128)(2,1)} %pack.1.own), channel_id=1, source_target_pairs={{0,1},{1,0},{2,3},{3,2},{4,5},{5,4},{6,7},{7,6},{8,9},{9,8},{10,11... | collective-permute-start | bytes 3538952 | tf_op jit(solution)/shard_map/ppermute | solution.py:34
  11.7 0.0 copy-start
  11.7 1.3 %copy-done = bf16[192,3072]{1,0:T(8,128)(2,1)S(1)} copy-done((bf16[192,3072]{1,0:T(8,128)(2,1)S(1)}, bf16[192,3072]{1,0:T(8,128)(2,1)}, u32[]{:S(2)}) %copy-start) | copy-done | bytes 1179672
  13.0 0.6 own_product.1.before
  13.6 0.8 %collective-permute-done.other = bf16[192,3072]{1,0:T(8,128)(2,1)S(1)} collective-permute-done((bf16[192,3072]{1,0:T(8,128)(2,1)}, bf16[192,3072]{1,0:T(8,128)(2,1)S(1)}, u32[]{:S(2)}, u32[]{:S(2)}) %collective-permute-start) | collective-permute-done | bytes 1179680 | tf_op jit(solution)/shard_map/ppermute | solution.py:34
  14.4 1.9 %pair_product.1 = bf16[2560,256]{1,0:T(8,128)(2,1)} custom-call(bf16[192,3072]{1,0:T(8,128)(2,1)S(1)} %collective-permute-done.other, f32[4,2,640,128]{3,2,1,0:T(8,128)S(1)} %own_product.1.before), custom_call_target="tpu_custom_call" | custom-call | tf_op jit(solution)/shard_map/pair_product/pallas_call | solution.py:167
  16.3 0.0 copy-start.2
  16.3 6.2 %all-to-all-start = ((bf16[16,160,256]{2,1,0:T(8,128)(2,1)}), bf16[16,160,256]{2,1,0:T(8,128)(2,1)S(1)}, u32[]{:S(2)}, u32[]{:S(2)}) async-start(bf16[16,160,256]{2,1,0:T(8,128)(2,1)} %bitcast.after), calls=%async_computation | async-start | bytes 2621440 | tf_op jit(solution)/shard_map/all_to_all | solution.py:30
  22.5 0.0 copy-done.2
  22.5 15.7 %all_gather.3 = bf16[640,512]{1,0:T(8,128)(2,1)S(1)} all-gather(bf16[80,512]{1,0:T(8,128)(2,1)S(1)} %hold.1), channel_id=1, replica_groups=mesh['x'=4,'zh'=4,'zl'=4,'y'=4,'c'=2] {'zl','c'}, dimensions={0}, use_global_device_ids=true | all-gather | bytes 737280 | tf_op jit(solution)/shard_map/all_gather | solution.py:197
  38.3 2.5 %collective-permute-start.1 = (bf16[4,2,80,512]{3,2,1,0:T(8,128)(2,1)S(1)}, bf16[4,2,80,512]{3,2,1,0:T(8,128)(2,1)S(1)}, u32[]{:S(2)}, u32[]{:S(2)}) collective-permute-start(bf16[4,2,80,512]{3,2,1,0:T(8,128)(2,1)S(1)} %bitcast.2), channel_id=1, source_target_pairs={{2,0},{7,1},{4,2},{1,3},{6,4},{3,5},{0,6},{5,7},{10,8},{15,9},{12,... | collective-permute-start | bytes 1966088 | tf_op jit(solution)/shard_map/ppermute | solution.py:199
  40.8 0.0 copy-start.1
  40.8 3.0 %collective-permute-start.2 = (bf16[4,80,512]{2,1,0:T(8,128)(2,1)S(1)}, bf16[4,80,512]{2,1,0:T(8,128)(2,1)S(1)}, u32[]{:S(2)}, u32[]{:S(2)}) collective-permute-start(bf16[4,80,512]{2,1,0:T(8,128)(2,1)S(1)} %own_half.1), channel_id=1, source_target_pairs={{4,0},{5,1},{6,2},{7,3},{0,4},{1,5},{2,6},{3,7},{12,8},{13,9},{14,... | collective-permute-start | bytes 983048 | tf_op jit(solution)/shard_map/ppermute | solution.py:200
  43.8 0.0 all-to-all-done.parts
  43.9 1.0 %sum_chips.1 = bf16[32,8,256]{2,1,0:T(8,128)(2,1)} custom-call(bf16[16,160,256]{2,1,0:T(8,128)(2,1)S(1)} %all-to-all-done.parts), custom_call_target="tpu_custom_call" | custom-call | tf_op jit(solution)/shard_map/sum_chips/pallas_call | solution.py:202
  44.8 15.1 %all-to-all-start.1 = ((bf16[32,8,256]{2,1,0:T(8,128)(2,1)}), bf16[32,8,256]{2,1,0:T(8,128)(2,1)S(1)}, u32[]{:S(2)}, u32[]{:S(2)}) async-start(bf16[32,8,256]{2,1,0:T(8,128)(2,1)} %sum_chips.1), calls=%async_computation.1 | async-start | bytes 262144 | tf_op jit(solution)/shard_map/all_to_all | solution.py:30
  60.0 0.0 collective-permute-done.2.far
  60.0 2.3 %collective-permute-start.5 = (bf16[4,80,512]{2,1,0:T(8,128)(2,1)S(1)}, bf16[4,80,512]{2,1,0:T(8,128)(2,1)S(1)}, u32[]{:S(2)}, u32[]{:S(2)}) collective-permute-start(bf16[4,80,512]{2,1,0:T(8,128)(2,1)S(1)} %collective-permute-done.2.far), channel_id=1, source_target_pairs={{0,1},{1,0},{2,3},{3,2},{4,5},{5,4},{6,7},{7,6},{8,9},{9,8},{10,11... | collective-permute-start | bytes 983048 | tf_op jit(solution)/shard_map/ppermute | solution.py:34
  62.3 0.0 collective-permute-done.1.near
  62.3 2.1 %collective-permute-start.3 = (bf16[2,2,80,512]{3,2,1,0:T(8,128)(2,1)S(1)}, bf16[2,2,80,512]{3,2,1,0:T(8,128)(2,1)S(1)}, u32[]{:S(2)}, u32[]{:S(2)}) collective-permute-start(bf16[2,2,80,512]{3,2,1,0:T(8,128)(2,1)S(1)} %get-tuple-element.6), channel_id=1, source_target_pairs={{0,1},{1,0},{2,3},{3,2},{4,5},{5,4},{6,7},{7,6},{8,9},{9,8},{10,11... | collective-permute-start | bytes 983048 | tf_op jit(solution)/shard_map/ppermute | solution.py:34
  64.4 2.3 %collective-permute-start.4 = (bf16[2,2,80,512]{3,2,1,0:T(8,128)(2,1)S(1)}, bf16[2,2,80,512]{3,2,1,0:T(8,128)(2,1)S(1)}, u32[]{:S(2)}, u32[]{:S(2)}) collective-permute-start(bf16[2,2,80,512]{3,2,1,0:T(8,128)(2,1)S(1)} %get-tuple-element.7), channel_id=1, source_target_pairs={{0,1},{1,0},{2,3},{3,2},{4,5},{5,4},{6,7},{7,6},{8,9},{9,8},{10,11... | collective-permute-start | bytes 983048 | tf_op jit(solution)/shard_map/ppermute | solution.py:34
  66.7 0.0 collective-permute-done.5.far_other
  66.7 0.0 collective-permute-done.3.low
  66.7 1.2 %collective-permute-done.4.high = bf16[2,2,80,512]{3,2,1,0:T(8,128)(2,1)S(1)} collective-permute-done((bf16[2,2,80,512]{3,2,1,0:T(8,128)(2,1)S(1)}, bf16[2,2,80,512]{3,2,1,0:T(8,128)(2,1)S(1)}, u32[]{:S(2)}, u32[]{:S(2)}) %collective-permute-start.4) | collective-permute-done | bytes 327712 | tf_op jit(solution)/shard_map/ppermute | solution.py:34
  67.9 0.0 copy-done.1
  67.9 2.0 %input_product.1 = (bf16[192,2560]{1,0:T(8,128)(2,1)}, f32[8,128]{1,0:T(8,128)S(1)}) custom-call(bf16[192,512]{1,0:T(8,128)(2,1)S(1)} %copy-done.1, bf16[4,2,80,512]{3,2,1,0:T(8,128)(2,1)S(1)} %bitcast.4, bf16[4,2,80,512]{3,2,1,0:T(8,128)(2,1)S(1)} %collective-permute-done.1.near, bf16[4,80,512]{2,1,0:T(8,128)(2,1)S(1)} %collective-permute-done.2.far, ...), custom_call_target="tpu_custom_call" | custom-call | tf_op jit(solution)/shard_map/input_product/pallas_call | solution.py:212
  69.9 0.0 all-to-all-done.1.parts
  69.9 0.6 sum_planes.1
  (3 shorter events, 0.1 us)
Async XLA Ops:
  2.9 11.5 %collective-permute-start = (bf16[192,3072]{1,0:T(8,128)(2,1)}, bf16[192,3072]{1,0:T(8,128)(2,1)S(1)}, u32[]{:S(2)}, u32[]{:S(2)}) collective-permute-start(bf16[192,3072]{1,0:T(8,128)(2,1)} %pack.1.own), channel_id=1, source_target_pairs={{0,1},{1,0},{2,3},{3,2},{4,5},{5,4},{6,7},{7,6},{8,9},{9,8},{10,11... | collective-permute-start | bytes 3538952 | tf_op jit(solution)/shard_map/ppermute | solution.py:34
  11.7 1.3 %copy-start = (bf16[192,3072]{1,0:T(8,128)(2,1)S(1)}, bf16[192,3072]{1,0:T(8,128)(2,1)}, u32[]{:S(2)}) copy-start(bf16[192,3072]{1,0:T(8,128)(2,1)} %pack.1.own) | copy-start | bytes 3538948
  16.3 6.2 %copy-start.2 = (bf16[80,512]{1,0:T(8,128)(2,1)S(1)}, bf16[80,512]{1,0:T(8,128)(2,1)}, u32[]{:S(2)}) copy-start(bf16[80,512]{1,0:T(8,128)(2,1)} %weight.1) | copy-start | bytes 245764
  16.3 27.6 %all-to-all-start = ((bf16[16,160,256]{2,1,0:T(8,128)(2,1)}), bf16[16,160,256]{2,1,0:T(8,128)(2,1)S(1)}, u32[]{:S(2)}, u32[]{:S(2)}) async-start(bf16[16,160,256]{2,1,0:T(8,128)(2,1)} %bitcast.after), calls=%async_computation | async-start | bytes 2621440 | tf_op jit(solution)/shard_map/all_to_all | solution.py:30
  38.3 24.0 %collective-permute-start.1 = (bf16[4,2,80,512]{3,2,1,0:T(8,128)(2,1)S(1)}, bf16[4,2,80,512]{3,2,1,0:T(8,128)(2,1)S(1)}, u32[]{:S(2)}, u32[]{:S(2)}) collective-permute-start(bf16[4,2,80,512]{3,2,1,0:T(8,128)(2,1)S(1)} %bitcast.2), channel_id=1, source_target_pairs={{2,0},{7,1},{4,2},{1,3},{6,4},{3,5},{0,6},{5,7},{10,8},{15,9},{12,... | collective-permute-start | bytes 1966088 | tf_op jit(solution)/shard_map/ppermute | solution.py:199
  40.8 27.1 %copy-start.1 = (bf16[192,512]{1,0:T(8,128)(2,1)S(1)}, bf16[192,512]{1,0:T(8,128)(2,1)}, u32[]{:S(2)}) copy-start(bf16[192,512]{1,0:T(8,128)(2,1)} %grad.3) | copy-start | bytes 589828
  40.8 19.2 %collective-permute-start.2 = (bf16[4,80,512]{2,1,0:T(8,128)(2,1)S(1)}, bf16[4,80,512]{2,1,0:T(8,128)(2,1)S(1)}, u32[]{:S(2)}, u32[]{:S(2)}) collective-permute-start(bf16[4,80,512]{2,1,0:T(8,128)(2,1)S(1)} %own_half.1), channel_id=1, source_target_pairs={{4,0},{5,1},{6,2},{7,3},{0,4},{1,5},{2,6},{3,7},{12,8},{13,9},{14,... | collective-permute-start | bytes 983048 | tf_op jit(solution)/shard_map/ppermute | solution.py:200
  44.8 25.1 %all-to-all-start.1 = ((bf16[32,8,256]{2,1,0:T(8,128)(2,1)}), bf16[32,8,256]{2,1,0:T(8,128)(2,1)S(1)}, u32[]{:S(2)}, u32[]{:S(2)}) async-start(bf16[32,8,256]{2,1,0:T(8,128)(2,1)} %sum_chips.1), calls=%async_computation.1 | async-start | bytes 262144 | tf_op jit(solution)/shard_map/all_to_all | solution.py:30
  60.0 6.7 %collective-permute-start.5 = (bf16[4,80,512]{2,1,0:T(8,128)(2,1)S(1)}, bf16[4,80,512]{2,1,0:T(8,128)(2,1)S(1)}, u32[]{:S(2)}, u32[]{:S(2)}) collective-permute-start(bf16[4,80,512]{2,1,0:T(8,128)(2,1)S(1)} %collective-permute-done.2.far), channel_id=1, source_target_pairs={{0,1},{1,0},{2,3},{3,2},{4,5},{5,4},{6,7},{7,6},{8,9},{9,8},{10,11... | collective-permute-start | bytes 983048 | tf_op jit(solution)/shard_map/ppermute | solution.py:34
  62.3 4.4 %collective-permute-start.3 = (bf16[2,2,80,512]{3,2,1,0:T(8,128)(2,1)S(1)}, bf16[2,2,80,512]{3,2,1,0:T(8,128)(2,1)S(1)}, u32[]{:S(2)}, u32[]{:S(2)}) collective-permute-start(bf16[2,2,80,512]{3,2,1,0:T(8,128)(2,1)S(1)} %get-tuple-element.6), channel_id=1, source_target_pairs={{0,1},{1,0},{2,3},{3,2},{4,5},{5,4},{6,7},{7,6},{8,9},{9,8},{10,11... | collective-permute-start | bytes 983048 | tf_op jit(solution)/shard_map/ppermute | solution.py:34
  64.4 3.5 %collective-permute-start.4 = (bf16[2,2,80,512]{3,2,1,0:T(8,128)(2,1)S(1)}, bf16[2,2,80,512]{3,2,1,0:T(8,128)(2,1)S(1)}, u32[]{:S(2)}, u32[]{:S(2)}) collective-permute-start(bf16[2,2,80,512]{3,2,1,0:T(8,128)(2,1)S(1)} %get-tuple-element.7), channel_id=1, source_target_pairs={{0,1},{1,0},{2,3},{3,2},{4,5},{5,4},{6,7},{7,6},{8,9},{9,8},{10,11... | collective-permute-start | bytes 983048 | tf_op jit(solution)/shard_map/ppermute | solution.py:34
